TPU v7x, 32 devices: a whole 2x2x4 slice. The times are simulated.
32 devices in a mesh: sp: 4 (over y, x), dp: 8 (over z, core).
Axes of the slice: x: 2, y: 2, z: 4, core: 2. Of those that a mesh axis runs over, the one named last changes fastest.
Arguments:
- tokens: bfloat16 [16, 1024, 1024], P('dp', 'sp'), may hold values from -6 to 6
- cotangent: bfloat16 [16, 1024, 1024], P('dp', 'sp'), may hold values from -6 to 6
- layer_norm_gain: float32 [2, 2, 1024], replicated, may hold values from 0.5 to 1.5
- layer_norm_bias: float32 [2, 2, 1024], replicated, may hold values from -1 to 1
- query_key_value_weight: bfloat16 [2, 1024, 3072], P(None, ('sp', 'dp')), may hold values from -0.1875 to 0.1875
- query_value_bias: float32 [2, 2, 1024], replicated, may hold values from -1.5 to 1.5
- attention_out_weight: bfloat16 [2, 1024, 1024], P(None, ('sp', 'dp')), may hold values from -0.75 to 0.75
- output_projection_bias: float32 [2, 2, 1024], replicated, may hold values from -1.5 to 1.5
- feed_up_weight: bfloat16 [2, 1024, 4096], P(None, ('sp', 'dp')), may hold values from -0.1875 to 0.1875
- feed_up_bias: float32 [2, 4096], replicated, may hold values from -1.5 to 1.5
- feed_down_weight: bfloat16 [2, 4096, 1024], P(None, ('sp', 'dp')), may hold values from -0.09375 to 0.09375
- adapter_down_maps: bfloat16 [2, 2, 1024, 4], replicated, may hold values from -0.1875 to 0.1875
- adapter_up_weights: bfloat16 [2, 2, 4, 1024], replicated, may hold values from -0.23925781 to 0.23925781
Outputs:
- layer_outputs: float32 [2, 16, 1024, 1024], P(None, 'dp', 'sp')
- grad_tokens: float32 [16, 1024, 1024], P('dp', 'sp')
- grad_lora_a: float32 [2, 2, 1024, 4], replicated
- grad_lora_b: float32 [2, 2, 4, 1024], replicated
All inputs are finite; a program needn't handle non-finite values.
Results may differ from a plain program's by a relative error of at most 0.014.
Values may be sent and summed in bfloat16 or wider, within the bound.
No kernel may reach another device: no remote copies, remote signals or barrier semaphores. Data moves between devices by JAX's collectives and lax.ppermute only.
A program may use at most 384 MiB of HBM per device.

v0:
```python
import jax
import jax.numpy as jnp
from jax import lax
from jax.sharding import PartitionSpec as P

HEAD = 64


adapter_scale = 8.0


def norm(hidden_state, norm_gain, bias):
    center = hidden_state - jnp.mean(hidden_state, axis=-1, keepdims=True)
    spread = jnp.mean(center * center, axis=-1, keepdims=True)
    return center * lax.rsqrt(spread + 1e-05) * norm_gain + bias


def smooth(value_rows):
    return jax.nn.gelu(value_rows, approximate=True)


def causal_mask(start, block, length):
    rows = lax.broadcasted_iota(jnp.int32, (block, length), 0) + start
    cols = lax.broadcasted_iota(jnp.int32, (block, length), 1)
    return cols <= rows


def attend(q_head, k_head, v_head):
    count, length, model_size = q_head.shape
    groups = model_size // HEAD
    q4 = q_head.reshape(count, length, groups, HEAD)
    k4 = k_head.reshape(count, length, groups, HEAD)
    v4 = v_head.reshape(count, length, groups, HEAD)
    block = min(512, length)
    mixed_docs = []
    lse_docs = []
    for index in range(count):
        k_doc = k4[index : index + 1]
        v_doc = v4[index : index + 1]
        mixed_parts = []
        lse_parts = []
        for start in range(0, length, block):
            q_block = q4[index : index + 1, start : start + block]
            scores = (
                jnp.einsum("nqhe,nkhe->nhqk", q_block, k_doc, preferred_element_type=jnp.float32)
                * 0.125
            )
            scores = jnp.where(causal_mask(start, block, length), scores, -1e30)
            top = jnp.max(scores, axis=-1, keepdims=True)
            weights = jnp.exp(scores - top)
            total = jnp.sum(weights, axis=-1, keepdims=True)
            probs = (weights / total).astype(jnp.bfloat16)
            lse_parts.append(top[..., 0] + jnp.log(total[..., 0]))
            part = jnp.einsum("nhqk,nkhe->nqhe", probs, v_doc, preferred_element_type=jnp.float32)
            mixed_parts.append(part.astype(jnp.bfloat16))
        mixed_docs.append(jnp.concatenate(mixed_parts, axis=1))
        lse_docs.append(jnp.concatenate(lse_parts, axis=2))
    mixed = jnp.concatenate(mixed_docs, axis=0).reshape(count, length, model_size)
    return (mixed, jnp.concatenate(lse_docs, axis=0))


def attend_back(q_head, k_head, v_head, lse, d_head):
    count, length, model_size = q_head.shape
    groups = model_size // HEAD
    q4 = q_head.reshape(count, length, groups, HEAD)
    k4 = k_head.reshape(count, length, groups, HEAD)
    v4 = v_head.reshape(count, length, groups, HEAD)
    d4 = d_head.reshape(count, length, groups, HEAD)
    block = min(512, length)
    grad_q_docs = []
    grad_k_docs = []
    grad_v_docs = []
    for index in range(count):
        k_doc = k4[index : index + 1]
        v_doc = v4[index : index + 1]
        grad_k = jnp.zeros(k_doc.shape, jnp.float32)
        grad_v = jnp.zeros(v_doc.shape, jnp.float32)
        grad_q_parts = []
        for start in range(0, length, block):
            q_block = q4[index : index + 1, start : start + block]
            d_block = d4[index : index + 1, start : start + block]
            scores = (
                jnp.einsum("nqhe,nkhe->nhqk", q_block, k_doc, preferred_element_type=jnp.float32)
                * 0.125
            )
            scores = jnp.where(causal_mask(start, block, length), scores, -1e30)
            probs = jnp.exp(scores - lse[index : index + 1, :, start : start + block, None])
            probs_low = probs.astype(jnp.bfloat16)
            d_probs = jnp.einsum(
                "nqhe,nkhe->nhqk", d_block, v_doc, preferred_element_type=jnp.float32
            )
            inner_sum = jnp.sum(probs * d_probs, axis=-1, keepdims=True)
            d_scores = (probs * (d_probs - inner_sum)).astype(jnp.bfloat16)
            grad_q_parts.append(
                jnp.einsum("nhqk,nkhe->nqhe", d_scores, k_doc, preferred_element_type=jnp.float32)
                * 0.125
            )
            grad_k = (
                grad_k
                + jnp.einsum(
                    "nhqk,nqhe->nkhe", d_scores, q_block, preferred_element_type=jnp.float32
                )
                * 0.125
            )
            grad_v = grad_v + jnp.einsum(
                "nhqk,nqhe->nkhe", probs_low, d_block, preferred_element_type=jnp.float32
            )
        grad_q_docs.append(jnp.concatenate(grad_q_parts, axis=1))
        grad_k_docs.append(grad_k)
        grad_v_docs.append(grad_v)
    array_shape = (count, length, model_size)
    grad_q = jnp.concatenate(grad_q_docs, axis=0)
    grad_k = jnp.concatenate(grad_k_docs, axis=0)
    grad_v = jnp.concatenate(grad_v_docs, axis=0)
    return (
        grad_q.reshape(array_shape).astype(jnp.bfloat16),
        grad_k.reshape(array_shape).astype(jnp.bfloat16),
        grad_v.reshape(array_shape).astype(jnp.bfloat16),
    )


def on_device(
    tokens,
    cotangent,
    layer_norm_gain,
    layer_norm_bias,
    query_key_value_weight,
    query_value_bias,
    attention_out_weight,
    output_projection_bias,
    feed_up_weight,
    feed_up_bias,
    feed_down_weight,
    adapter_down_maps,
    adapter_up_weights,
):
    layers = query_key_value_weight.shape[0]
    model_size = tokens.shape[2]
    adapter_width = adapter_down_maps.shape[3]

    def fetch(layer_index):
        return (
            lax.all_gather(query_key_value_weight[layer_index], ("sp", "dp"), axis=0, tiled=True),
            lax.all_gather(attention_out_weight[layer_index], ("sp", "dp"), axis=0, tiled=True),
            lax.all_gather(feed_up_weight[layer_index], ("sp", "dp"), axis=0, tiled=True),
            lax.all_gather(feed_down_weight[layer_index], ("sp", "dp"), axis=0, tiled=True),
        )

    stream = tokens.astype(jnp.float32)
    fetched = []
    saved = []
    outputs = []
    for layer_index in range(layers):
        mats = fetch(layer_index)
        qkv_full, out_full, up_full, down_full = mats
        fetched.append(mats)
        normed = norm(
            stream, layer_norm_gain[layer_index, 0], layer_norm_bias[layer_index, 0]
        ).astype(jnp.bfloat16)
        down_joined = jnp.concatenate(
            [adapter_down_maps[layer_index, 0], adapter_down_maps[layer_index, 1]], axis=1
        )
        base_output = jnp.dot(normed, qkv_full, preferred_element_type=jnp.float32)
        inner_hidden = jnp.dot(normed, down_joined, preferred_element_type=jnp.float32).astype(
            jnp.bfloat16
        )
        query_adapter_term = adapter_scale * jnp.dot(
            inner_hidden[..., :adapter_width],
            adapter_up_weights[layer_index, 0],
            preferred_element_type=jnp.float32,
        )
        value_adapter_term = adapter_scale * jnp.dot(
            inner_hidden[..., adapter_width:],
            adapter_up_weights[layer_index, 1],
            preferred_element_type=jnp.float32,
        )
        query_rows = (
            base_output[..., :model_size] + query_value_bias[layer_index, 0] + query_adapter_term
        ).astype(jnp.bfloat16)
        keys = base_output[..., model_size : 2 * model_size].astype(jnp.bfloat16)
        value_rows = (
            base_output[..., 2 * model_size :]
            + query_value_bias[layer_index, 1]
            + value_adapter_term
        ).astype(jnp.bfloat16)
        q_head, k_head, v_head = (
            lax.all_to_all(query_rows, "sp", split_axis=2, concat_axis=1, tiled=True),
            lax.all_to_all(keys, "sp", split_axis=2, concat_axis=1, tiled=True),
            lax.all_to_all(value_rows, "sp", split_axis=2, concat_axis=1, tiled=True),
        )
        mixed, lse = attend(q_head, k_head, v_head)
        mixed_seq = lax.all_to_all(mixed, "sp", split_axis=1, concat_axis=2, tiled=True)
        middle = stream + (
            jnp.dot(mixed_seq, out_full, preferred_element_type=jnp.float32)
            + output_projection_bias[layer_index, 0]
        )
        second = norm(
            middle, layer_norm_gain[layer_index, 1], layer_norm_bias[layer_index, 1]
        ).astype(jnp.bfloat16)
        pre = (
            jnp.dot(second, up_full, preferred_element_type=jnp.float32) + feed_up_bias[layer_index]
        )
        acted = smooth(pre).astype(jnp.bfloat16)
        after = middle + (
            jnp.dot(acted, down_full, preferred_element_type=jnp.float32)
            + output_projection_bias[layer_index, 1]
        )
        saved.append((stream, normed, inner_hidden, q_head, k_head, v_head, lse, middle, pre))
        outputs.append(after)
        stream = after
    grad = cotangent.astype(jnp.float32)
    grads_a = []
    grads_b = []
    for layer_index in reversed(range(layers)):
        mats = fetch(layer_index)
        qkv_full, out_full, up_full, down_full = mats
        stream_in, normed, inner_hidden, q_head, k_head, v_head, lse, middle, pre = saved[
            layer_index
        ]
        d_acted = jnp.einsum(
            "nsd,fd->nsf", grad.astype(jnp.bfloat16), down_full, preferred_element_type=jnp.float32
        )
        unused, gelu_pull = jax.vjp(smooth, pre)
        d_pre = gelu_pull(d_acted)[0].astype(jnp.bfloat16)
        d_second = jnp.einsum("nsf,df->nsd", d_pre, up_full, preferred_element_type=jnp.float32)
        gain_two = layer_norm_gain[layer_index, 1]
        shift_two = layer_norm_bias[layer_index, 1]
        unused, second_pull = jax.vjp(lambda value: norm(value, gain_two, shift_two), middle)
        grad_mid = grad + second_pull(d_second)[0]
        d_mixed = jnp.einsum(
            "nse,de->nsd",
            grad_mid.astype(jnp.bfloat16),
            out_full,
            preferred_element_type=jnp.float32,
        ).astype(jnp.bfloat16)
        d_head = lax.all_to_all(d_mixed, "sp", split_axis=2, concat_axis=1, tiled=True)
        grad_q, grad_k, grad_v = attend_back(q_head, k_head, v_head, lse, d_head)
        query_gradient_rows, dk_seq, value_gradient_rows = (
            lax.all_to_all(grad_q, "sp", split_axis=1, concat_axis=2, tiled=True),
            lax.all_to_all(grad_k, "sp", split_axis=1, concat_axis=2, tiled=True),
            lax.all_to_all(grad_v, "sp", split_axis=1, concat_axis=2, tiled=True),
        )
        query_up_gradient = adapter_scale * jnp.einsum(
            "nsr,nsd->rd",
            inner_hidden[..., :adapter_width],
            query_gradient_rows,
            preferred_element_type=jnp.float32,
        )
        value_up_gradient = adapter_scale * jnp.einsum(
            "nsr,nsd->rd",
            inner_hidden[..., adapter_width:],
            value_gradient_rows,
            preferred_element_type=jnp.float32,
        )
        d_inner = jnp.concatenate(
            [
                adapter_scale
                * jnp.einsum(
                    "jmw,qw->jmq",
                    query_gradient_rows,
                    adapter_up_weights[layer_index, 0],
                    preferred_element_type=jnp.float32,
                ),
                adapter_scale
                * jnp.einsum(
                    "jmw,qw->jmq",
                    value_gradient_rows,
                    adapter_up_weights[layer_index, 1],
                    preferred_element_type=jnp.float32,
                ),
            ],
            axis=-1,
        ).astype(jnp.bfloat16)
        grad_down = jnp.einsum("nsd,nsr->dr", normed, d_inner, preferred_element_type=jnp.float32)
        down_joined = jnp.concatenate(
            [adapter_down_maps[layer_index, 0], adapter_down_maps[layer_index, 1]], axis=1
        )
        d_all = jnp.concatenate([query_gradient_rows, dk_seq, value_gradient_rows], axis=-1)
        d_normed = jnp.einsum("nse,de->nsd", d_all, qkv_full, preferred_element_type=jnp.float32)
        d_normed = d_normed + jnp.einsum(
            "nsr,dr->nsd", d_inner, down_joined, preferred_element_type=jnp.float32
        )
        gain_one = layer_norm_gain[layer_index, 0]
        shift_one = layer_norm_bias[layer_index, 0]
        unused, first_pull = jax.vjp(lambda value: norm(value, gain_one, shift_one), stream_in)
        grad = grad_mid + first_pull(d_normed)[0]
        grads_a.append(jnp.stack([grad_down[:, :adapter_width], grad_down[:, adapter_width:]]))
        grads_b.append(jnp.stack([query_up_gradient, value_up_gradient]))
    total_a, total_b = lax.psum((jnp.stack(grads_a[::-1]), jnp.stack(grads_b[::-1])), ("sp", "dp"))
    return (jnp.stack(outputs), grad, total_a, total_b)


def solution(mesh):
    in_specs = (
        P("dp", "sp", None),
        P("dp", "sp", None),
        P(),
        P(),
        P(None, ("sp", "dp"), None),
        P(),
        P(None, ("sp", "dp"), None),
        P(),
        P(None, ("sp", "dp"), None),
        P(),
        P(None, ("sp", "dp"), None),
        P(),
        P(),
    )
    out_specs = (P(None, "dp", "sp", None), P("dp", "sp", None), P(), P())
    return jax.shard_map(
        on_device, mesh=mesh, in_specs=in_specs, out_specs=out_specs, check_vma=False
    )
```

profile of v0, /device:TPU:0, one launch (start us, length us, event | category | flops | bytes accessed | tf_op | source)
XLA Modules:
  0.0 1102.7 jit_solution(7521749069584492741)
XLA Ops:
  22.1 61.7 %all-gather.17.cloned.1.call-done = bf16[1,1024,3072]{2,1,0:T(8,128)(2,1)} async-done(((bf16[1,32,3072]{2,1,0:T(8,128)(2,1)}), bf16[1,1024,3072]{2,1,0:T(8,128)(2,1)}) %all-gather.17.cloned.1.call-update) | async-done | bytes 6291472 | tf_op jit(solution)/shard_map/all_gather | solution.py:143
  105.6 7.0 all-to-all-done.1
  143.1 6.1 fusion.340
  199.5 20.5 %all-to-all-done.3 = bf16[2,1024,256]{2,0,1:T(2,128)(2,1)S(1)} async-done(((bf16[2,1024,256]{2,0,1:T(2,128)(2,1)}), bf16[2,1024,256]{2,0,1:T(2,128)(2,1)S(1)}, u32[]{:S(2)}, u32[]{:S(2)}) %all-to-all-start.3) | async-done | bytes 1048608 | tf_op jit(solution)/shard_map/all_to_all | solution.py:192
  232.8 12.0 %fusion.28 = f32[2,256,4096]{2,1,0:T(8,128)} fusion(bf16[1,1024,4096]{2,1,0:T(8,128)(2,1)} %all-gather.21.cloned.1.call-done, f32[2,256,1024]{2,1,0:T(8,128)} %copy-done.37, f32[1024]{0:T(1024)S(1)} %bitcast.635, f32[1024]{0:T(1024)S(1)} %bitcast.619, f32[2,256]{1,0:T(2,128)S(1)} %fusion.306, f32[2,256]{1,0:T(2,128)S(1)} %broadcast_multiply_fusion.2), kind=kOutput, calls=%fused_computation.32 | convolution fusion | flops 4297588736 | bytes 18886656 | tf_op jit(solution)/shard_map/dot_general | solution.py:201
  244.8 66.1 %all-gather.23.cloned.1.call-done = bf16[1,4096,1024]{2,1,0:T(8,128)(2,1)} async-done(((bf16[1,128,1024]{2,1,0:T(8,128)(2,1)}), bf16[1,4096,1024]{2,1,0:T(8,128)(2,1)}) %all-gather.23.cloned.1.call-update) | async-done | bytes 8388624 | tf_op jit(solution)/shard_map/all_gather | solution.py:146
  310.9 10.6 fusion.345
  323.7 58.2 %all-gather.25.cloned.1.call-done = bf16[1,1024,3072]{2,1,0:T(8,128)(2,1)} async-done(((bf16[1,32,3072]{2,1,0:T(8,128)(2,1)}), bf16[1,1024,3072]{2,1,0:T(8,128)(2,1)}) %all-gather.25.cloned.1.call-update) | async-done | bytes 6291472 | tf_op jit(solution)/shard_map/all_gather | solution.py:143
  400.7 10.1 all-to-all-done.5
  420.8 8.0 all-to-all-done.4
  485.4 16.7 %all-to-all-done.7 = bf16[2,1024,256]{2,0,1:T(2,128)(2,1)S(1)} async-done(((bf16[2,1024,256]{2,0,1:T(2,128)(2,1)}), bf16[2,1024,256]{2,0,1:T(2,128)(2,1)S(1)}, u32[]{:S(2)}, u32[]{:S(2)}) %all-to-all-start.7) | async-done | bytes 1048608 | tf_op jit(solution)/shard_map/all_to_all | solution.py:192
  510.5 13.4 %all-gather.29.cloned.1.call-done = bf16[1,1024,4096]{2,1,0:T(8,128)(2,1)} async-done(((bf16[1,32,4096]{2,1,0:T(8,128)(2,1)}), bf16[1,1024,4096]{2,1,0:T(8,128)(2,1)}) %all-gather.29.cloned.1.call-update) | async-done | bytes 8388624 | tf_op jit(solution)/shard_map/all_gather | solution.py:145
  523.9 12.1 %fusion.20 = f32[2,256,4096]{2,1,0:T(8,128)} fusion(bf16[1,1024,4096]{2,1,0:T(8,128)(2,1)} %all-gather.29.cloned.1.call-done, f32[2,256,1024]{2,1,0:T(8,128)} %copy-done.40, f32[1024]{0:T(1024)S(1)} %bitcast.633, f32[1024]{0:T(1024)S(1)} %bitcast.622, f32[2,256]{1,0:T(2,128)S(1)} %fusion.308, f32[2,256]{1,0:T(2,128)S(1)} %broadcast_multiply_fusion), kind=kOutput, calls=%fused_computation.24 | convolution fusion | flops 4297588736 | bytes 18886656 | tf_op jit(solution)/shard_map/dot_general | solution.py:201
  536.0 67.0 %all-gather.31.cloned.1.call-done = bf16[1,4096,1024]{2,1,0:T(8,128)(2,1)} async-done(((bf16[1,128,1024]{2,1,0:T(8,128)(2,1)}), bf16[1,4096,1024]{2,1,0:T(8,128)(2,1)}) %all-gather.31.cloned.1.call-update) | async-done | bytes 8388624 | tf_op jit(solution)/shard_map/all_gather | solution.py:146
  603.0 15.2 %fusion.13 = bf16[2,256,4096]{2,1,0:T(8,128)(2,1)} fusion(f32[2,256,4096]{2,1,0:T(8,128)} %fusion.20, bf16[2,256,1024]{2,1,0:T(8,128)(2,1)S(1)} %copy-done.61, bf16[1,4096,1024]{2,1,0:T(8,128)(2,1)} %all-gather.31.cloned.1.call-done, f32[4096]{0:T(1024)S(1)} %bitcast.617), kind=kOutput, calls=%fused_computation.17 | convolution fusion | flops 4339007488 | bytes 22036480 | tf_op jit(solution)/shard_map/nsd,fd->nsf/dot_general | solution.py:220
  618.2 7.1 multiply_reduce_fusion.10
  636.9 14.2 %all-to-all-done.8 = bf16[2,256,1024]{1,0,2:T(2,128)(2,1)S(1)} async-done(((bf16[2,256,1024]{1,0,2:T(2,128)(2,1)}), bf16[2,256,1024]{1,0,2:T(2,128)(2,1)S(1)}, u32[]{:S(2)}, u32[]{:S(2)}) %all-to-all-start.8) | async-done | bytes 1048608 | tf_op jit(solution)/shard_map/all_to_all | solution.py:236
  659.8 6.7 multiply_reduce_fusion.4
  692.3 6.8 multiply_convert_fusion.4
  701.3 7.4 multiply_convert_fusion.5
  744.5 7.0 all-to-all-done.9
  756.0 13.1 %add_bitcast_fusion = f32[1,2,256,1024]{3,2,1,0:T(8,128)} fusion(f32[2,256,1024]{2,1,0:T(8,128)} %copy-done.40, bf16[1,4096,1024]{2,1,0:T(8,128)(2,1)} %all-gather.31.cloned.1.call-done, f32[2,256,4096]{2,1,0:T(8,128)} %fusion.20, f32[4096]{0:T(1024)S(1)} %bitcast.618, f32[1024]{0:T(1024)S(1)} %bitcast.632), kind=kOutput, calls=%fused_computation.200 | convolution fusion | flops 4316987392 | bytes 20992000 | tf_op jit(solution)/shard_map/dot_general | solution.py:205
  788.5 7.3 multiply_reduce_fusion.9
  797.3 13.5 %fusion.6 = bf16[2,256,4096]{2,1,0:T(8,128)(2,1)S(1)} fusion(f32[2,256,4096]{2,1,0:T(8,128)} %fusion.28, bf16[1,4096,1024]{2,1,0:T(8,128)(2,1)} %all-gather.23.cloned.1.call-done, f32[4096]{0:T(1024)S(1)} %bitcast.616, f32[2,256,1024]{2,1,0:T(8,128)S(1)} %add_add_fusion.6), kind=kOutput, calls=%fused_computation.10 | convolution fusion | flops 4339531776 | bytes 23085056 | tf_op jit(solution)/shard_map/nsd,fd->nsf/dot_general | solution.py:220
  810.9 7.1 multiply_reduce_fusion.8
  835.6 8.1 all-to-all-done.12
  846.6 6.2 fusion.58
  852.9 6.7 multiply_reduce_fusion
  889.5 6.9 multiply_convert_fusion
  898.5 7.4 multiply_convert_fusion.2
  960.6 7.3 fusion.118
  976.3 116.5 %all-reduce.3.cloned.1.call-done = (f32[2,2,1024,4]{2,3,1,0:T(4,128)}, f32[2,2,4,1024]{3,2,1,0:T(4,128)}) async-done(((f32[2,2,1024,4]{2,3,1,0:T(4,128)}, f32[2,2,4,1024]{3,2,1,0:T(4,128)}), (f32[2,2,1024,4]{2,3,1,0:T(4,128)}, f32[2,2,4,1024]{3,2,1,0:T(4,128)})) %all-reduce.3.cloned.1.call-update) | async-done | bytes 131088 | tf_op jit(solution)/shard_map/psum | solution.py:289
  (558 shorter events, 451.6 us)
Async XLA Ops:
  7.2 76.7 %all-gather.17.cloned.1.call-start = ((), (), s32[]{:S(2)}) async-start(), calls=%async_computation.16 | async-start | bytes 6488064 | tf_op jit(solution)/shard_map/all_gather | solution.py:143
  9.1 214.5 %all-gather.19.cloned.1.call-start = ((), (), s32[]{:S(2)}) async-start(), calls=%async_computation.17 | async-start | bytes 2162688 | tf_op jit(solution)/shard_map/all_gather | solution.py:144
  10.8 222.1 %all-gather.21.cloned.1.call-start = ((), (), s32[]{:S(2)}) async-start(), calls=%async_computation.18 | async-start | bytes 8650752 | tf_op jit(solution)/shard_map/all_gather | solution.py:145
  12.7 298.2 %all-gather.23.cloned.1.call-start = ((), (), s32[]{:S(2)}) async-start(), calls=%async_computation.19 | async-start | bytes 8650752 | tf_op jit(solution)/shard_map/all_gather | solution.py:146
  14.6 367.2 %all-gather.25.cloned.1.call-start = ((), (), s32[]{:S(2)}) async-start(), calls=%async_computation.20 | async-start | bytes 6488064 | tf_op jit(solution)/shard_map/all_gather | solution.py:143
  15.2 490.6 %all-gather.27.cloned.1.call-start = ((), (), s32[]{:S(2)}) async-start(), calls=%async_computation.21 | async-start | bytes 2162688 | tf_op jit(solution)/shard_map/all_gather | solution.py:144
  15.8 508.0 %all-gather.29.cloned.1.call-start = ((), (), s32[]{:S(2)}) async-start(), calls=%async_computation.22 | async-start | bytes 8650752 | tf_op jit(solution)/shard_map/all_gather | solution.py:145
  20.3 212.5 %copy-start.107 = (f32[1,1,1024]{2,1,0:T(1,128)}, f32[1,1,1024]{2,1,0:T(1,128)S(1)}, u32[]{:S(2)}) copy-start(f32[1,1,1024]{2,1,0:T(1,128)S(1)} %get-tuple-element.41) | copy-start | bytes 12292
  20.3 301.6 %copy-start.99 = (f32[1,1,1024]{2,1,0:T(1,128)}, f32[1,1,1024]{2,1,0:T(1,128)S(1)}, u32[]{:S(2)}) copy-start(f32[1,1,1024]{2,1,0:T(1,128)S(1)} %get-tuple-element.43) | copy-start | bytes 12292
  21.0 302.3 %copy-start.73 = (bf16[1024,4]{0,1:T(4,128)(2,1)}, bf16[1024,4]{0,1:T(4,128)(2,1)S(1)}, u32[]{:S(2)}) copy-start(bf16[1024,4]{0,1:T(4,128)(2,1)S(1)} %get-tuple-element.32) | copy-start | bytes 24580
  21.0 302.3 %copy-start.75 = (bf16[1024,4]{0,1:T(4,128)(2,1)}, bf16[1024,4]{0,1:T(4,128)(2,1)S(1)}, u32[]{:S(2)}) copy-start(bf16[1024,4]{0,1:T(4,128)(2,1)S(1)} %get-tuple-element.35) | copy-start | bytes 24580
  22.1 95.8 %copy-start.71 = (bf16[2,256,8]{1,2,0:T(8,128)(2,1)}, bf16[2,256,8]{1,2,0:T(8,128)(2,1)S(1)}, u32[]{:S(2)}) copy-start(bf16[2,256,8]{1,2,0:T(8,128)(2,1)S(1)} %convolution_convert_fusion.1) | copy-start | bytes 24580
  94.8 17.8 %all-to-all-start.1 = ((bf16[2,256,1024]{1,0,2:T(2,128)(2,1)}), bf16[2,256,1024]{1,0,2:T(2,128)(2,1)S(1)}, u32[]{:S(2)}, u32[]{:S(2)}) async-start(bf16[2,256,1024]{1,0,2:T(2,128)(2,1)} %copy.39), calls=%async_computation.1 | async-start | bytes 2097152 | tf_op jit(solution)/shard_map/all_to_all | solution.py:187
  98.3 504.6 %all-gather.31.cloned.1.call-start = ((), (), s32[]{:S(2)}) async-start(), calls=%async_computation.23 | async-start | bytes 8650752 | tf_op jit(solution)/shard_map/all_gather | solution.py:146
  112.7 19.5 %all-to-all-start.2 = ((bf16[2,256,1024]{1,0,2:T(2,128)(2,1)}), bf16[2,256,1024]{1,0,2:T(2,128)(2,1)}, u32[]{:S(2)}, u32[]{:S(2)}) async-start(bf16[2,256,1024]{1,0,2:T(2,128)(2,1)} %copy.41), calls=%async_computation.2 | async-start | bytes 2097152 | tf_op jit(solution)/shard_map/all_to_all | solution.py:188
  132.2 31.8 %all-to-all-start = ((bf16[2,256,1024]{1,0,2:T(2,128)(2,1)}), bf16[2,256,1024]{1,0,2:T(2,128)(2,1)}, u32[]{:S(2)}, u32[]{:S(2)}) async-start(bf16[2,256,1024]{1,0,2:T(2,128)(2,1)} %copy.37), calls=%async_computation | async-start | bytes 2097152 | tf_op jit(solution)/shard_map/all_to_all | solution.py:189
  195.1 24.9 %all-to-all-start.3 = ((bf16[2,1024,256]{2,0,1:T(2,128)(2,1)}), bf16[2,1024,256]{2,0,1:T(2,128)(2,1)S(1)}, u32[]{:S(2)}, u32[]{:S(2)}) async-start(bf16[2,1024,256]{2,0,1:T(2,128)(2,1)} %copy.43), calls=%async_computation.3 | async-start | bytes 2097152 | tf_op jit(solution)/shard_map/all_to_all | solution.py:192
  199.5 111.5 %copy-start.105 = (f32[1,4096]{1,0:T(1,128)}, f32[1,4096]{1,0:T(1,128)S(1)}, u32[]{:S(2)}) copy-start(f32[1,4096]{1,0:T(1,128)S(1)} %get-tuple-element.31) | copy-start | bytes 49156
  392.6 18.2 %all-to-all-start.5 = ((bf16[2,256,1024]{1,0,2:T(2,128)(2,1)}), bf16[2,256,1024]{1,0,2:T(2,128)(2,1)S(1)}, u32[]{:S(2)}, u32[]{:S(2)}) async-start(bf16[2,256,1024]{1,0,2:T(2,128)(2,1)} %copy.47), calls=%async_computation.5 | async-start | bytes 2097152 | tf_op jit(solution)/shard_map/all_to_all | solution.py:187
  410.9 18.0 %all-to-all-start.4 = ((bf16[2,256,1024]{1,0,2:T(2,128)(2,1)}), bf16[2,256,1024]{1,0,2:T(2,128)(2,1)S(1)}, u32[]{:S(2)}, u32[]{:S(2)}) async-start(bf16[2,256,1024]{1,0,2:T(2,128)(2,1)} %copy.45), calls=%async_computation.4 | async-start | bytes 2097152 | tf_op jit(solution)/shard_map/all_to_all | solution.py:189
  428.8 16.4 %all-to-all-start.6 = ((bf16[2,256,1024]{1,0,2:T(2,128)(2,1)}), bf16[2,256,1024]{1,0,2:T(2,128)(2,1)}, u32[]{:S(2)}, u32[]{:S(2)}) async-start(bf16[2,256,1024]{1,0,2:T(2,128)(2,1)} %copy.49), calls=%async_computation.6 | async-start | bytes 2097152 | tf_op jit(solution)/shard_map/all_to_all | solution.py:188
  479.5 22.6 %all-to-all-start.7 = ((bf16[2,1024,256]{2,0,1:T(2,128)(2,1)}), bf16[2,1024,256]{2,0,1:T(2,128)(2,1)S(1)}, u32[]{:S(2)}, u32[]{:S(2)}) async-start(bf16[2,1024,256]{2,0,1:T(2,128)(2,1)} %copy.51), calls=%async_computation.7 | async-start | bytes 2097152 | tf_op jit(solution)/shard_map/all_to_all | solution.py:192
  523.9 79.1 %copy-start.61 = (bf16[2,256,1024]{2,1,0:T(8,128)(2,1)S(1)}, bf16[2,256,1024]{2,1,0:T(8,128)(2,1)}, u32[]{:S(2)}) copy-start(bf16[2,256,1024]{2,1,0:T(8,128)(2,1)} %param.14) | copy-start | bytes 3145732
  633.3 17.8 %all-to-all-start.8 = ((bf16[2,256,1024]{1,0,2:T(2,128)(2,1)}), bf16[2,256,1024]{1,0,2:T(2,128)(2,1)S(1)}, u32[]{:S(2)}, u32[]{:S(2)}) async-start(bf16[2,256,1024]{1,0,2:T(2,128)(2,1)} %copy.53), calls=%async_computation.8 | async-start | bytes 2097152 | tf_op jit(solution)/shard_map/all_to_all | solution.py:236
  687.9 45.8 %all-to-all-start.11 = ((bf16[2,1024,256]{2,0,1:T(2,128)(2,1)}), bf16[2,1024,256]{2,0,1:T(2,128)(2,1)}, u32[]{:S(2)}, u32[]{:S(2)}) async-start(bf16[2,1024,256]{2,0,1:T(2,128)(2,1)} %copy.59), calls=%async_computation.11 | async-start | bytes 2097152 | tf_op jit(solution)/shard_map/all_to_all | solution.py:241
  733.6 17.8 %all-to-all-start.9 = ((bf16[2,1024,256]{2,0,1:T(2,128)(2,1)}), bf16[2,1024,256]{2,0,1:T(2,128)(2,1)}, u32[]{:S(2)}, u32[]{:S(2)}) async-start(bf16[2,1024,256]{2,0,1:T(2,128)(2,1)} %copy.55), calls=%async_computation.9 | async-start | bytes 2097152 | tf_op jit(solution)/shard_map/all_to_all | solution.py:239
  751.5 30.4 %all-to-all-start.10 = ((bf16[2,1024,256]{2,0,1:T(2,128)(2,1)}), bf16[2,1024,256]{2,0,1:T(2,128)(2,1)}, u32[]{:S(2)}, u32[]{:S(2)}) async-start(bf16[2,1024,256]{2,0,1:T(2,128)(2,1)} %copy.57), calls=%async_computation.10 | async-start | bytes 2097152 | tf_op jit(solution)/shard_map/all_to_all | solution.py:240
  826.1 17.7 %all-to-all-start.12 = ((bf16[2,256,1024]{1,0,2:T(2,128)(2,1)}), bf16[2,256,1024]{1,0,2:T(2,128)(2,1)}, u32[]{:S(2)}, u32[]{:S(2)}) async-start(bf16[2,256,1024]{1,0,2:T(2,128)(2,1)} %copy.61), calls=%async_computation.12 | async-start | bytes 2097152 | tf_op jit(solution)/shard_map/all_to_all | solution.py:236
  885.0 35.0 %all-to-all-start.15 = ((bf16[2,1024,256]{2,0,1:T(2,128)(2,1)}), bf16[2,1024,256]{2,0,1:T(2,128)(2,1)}, u32[]{:S(2)}, u32[]{:S(2)}) async-start(bf16[2,1024,256]{2,0,1:T(2,128)(2,1)} %copy.67), calls=%async_computation.15 | async-start | bytes 2097152 | tf_op jit(solution)/shard_map/all_to_all | solution.py:241
  920.0 17.6 %all-to-all-start.13 = ((bf16[2,1024,256]{2,0,1:T(2,128)(2,1)}), bf16[2,1024,256]{2,0,1:T(2,128)(2,1)}, u32[]{:S(2)}, u32[]{:S(2)}) async-start(bf16[2,1024,256]{2,0,1:T(2,128)(2,1)} %copy.63), calls=%async_computation.13 | async-start | bytes 2097152 | tf_op jit(solution)/shard_map/all_to_all | solution.py:239
  937.6 17.4 %all-to-all-start.14 = ((bf16[2,1024,256]{2,0,1:T(2,128)(2,1)}), bf16[2,1024,256]{2,0,1:T(2,128)(2,1)}, u32[]{:S(2)}, u32[]{:S(2)}) async-start(bf16[2,1024,256]{2,0,1:T(2,128)(2,1)} %copy.65), calls=%async_computation.14 | async-start | bytes 2097152 | tf_op jit(solution)/shard_map/all_to_all | solution.py:240
  941.9 150.9 %all-reduce.3.cloned.1.call-start = ((), (), s32[]{:S(2)}) async-start(), calls=%async_computation.24 | async-start | bytes 262144 | tf_op jit(solution)/shard_map/psum | solution.py:289
  (141 other events, 1789.4 us)
Sparse Core Ops, SparseCore 0:
  11.6 72.2 all-gather.16
  87.4 54.9 all-gather.18
  145.4 87.3 all-gather.20
  235.6 75.2 all-gather.22
  313.8 68.0 all-gather.24
  385.3 54.9 all-gather.26
  443.3 80.5 all-gather.28
  526.8 76.0 all-gather.30
  971.4 121.3 all-reduce.2
where the time goes:
time: 1110 us; the launch traced here: 1100 us
  waiting for transfers between devices  500 us (45%)
  matrix products  282 us (25%)
  local copies, waits for them, and re-layouts  153 us (14%)
  other arithmetic  83.8 us (8%)
  starting transfers between devices  66.4 us (6%)
  between operations  16.8 us (2%)
    all_gather x2, waiting for transfers between devices, fetch(): lax.all_gather(feed_down_weight[layer_index], ('sp', 'dp'), axis=0, tiled...  133 us
    all_gather x2, waiting for transfers between devices, fetch(): lax.all_gather(query_key_value_weight[layer_index], ('sp', 'dp'), axis=0,...  120 us
    psum x1, waiting for transfers between devices, on_device(): lax.psum((jnp.stack(grads_a[::-1]), jnp.stack(grads_b[::-1])), ('sp', 'dp'))  117 us
    convert_element_type x8, other arithmetic, attend_back(): d_scores = (probs * (d_probs - inner_sum)).astype(jnp.bfloat16)  42.3 us
    dot_general x8, matrix products, attend_back(): jnp.einsum('nqhe,nkhe->nhqk', d_block, v_doc, preferred_element_type=jnp....  39.4 us
    all_to_all x2, waiting for transfers between devices, on_device(): lax.all_to_all(mixed, 'sp', split_axis=1, concat_axis=2, tiled=True)  37.2 us
    dot_general x8, matrix products, attend(): jnp.einsum('nqhe,nkhe->nhqk', q_block, k_doc, preferred_element_type=jnp....  30.6 us
    dot_general x2, matrix products, on_device(): jnp.einsum('nsd,fd->nsf', grad.astype(jnp.bfloat16), down_full, preferred...  28.7 us
  transfers between devices with their start and end apart: 25, of which 19 were waited for; matrix products, arithmetic and copies ran while one was open for 29% of the time, Pallas kernels for 0%

commit v1 on v0

v1 whole, which is shorter than its diff:
```python
import functools
import jax
import jax.numpy as jnp
from jax import lax
from jax.experimental import pallas as pl
from jax.experimental.pallas import tpu as pltpu
from jax.sharding import PartitionSpec as P

HEAD = 64
LANES = 128
adapter_scale = 8.0
VMEM_BYTES = 58 * 1024 * 1024
low = jnp.bfloat16
full = jnp.float32


def dot(left, right):
    return jnp.dot(left, right, preferred_element_type=full)


def dot_nt(left, right):
    return lax.dot_general(left, right, (((1,), (1,)), ((), ())), preferred_element_type=full)


def dot_tn(left, right):
    return lax.dot_general(left, right, (((0,), (0,)), ((), ())), preferred_element_type=full)


def normalise(value):
    center = value - jnp.mean(value, axis=-1, keepdims=True)
    scale = lax.rsqrt(jnp.mean(center * center, axis=-1, keepdims=True) + 1e-05)
    return center * scale, scale


def norm_back(unit, scale, gain, grad):
    grad = grad * gain
    inner = jnp.mean(grad * unit, axis=-1, keepdims=True)
    return scale * (grad - jnp.mean(grad, axis=-1, keepdims=True) - unit * inner)


def vmem():
    return pl.BlockSpec(memory_space=pltpu.VMEM)


def hbm():
    return pl.BlockSpec(memory_space=pl.ANY)


def smem():
    return pl.BlockSpec(memory_space=pltpu.SMEM)


def params():
    return pltpu.CompilerParams(vmem_limit_bytes=VMEM_BYTES)


class Loads:
    def __init__(self, pieces, column, offsets, first, target, sems, parts):
        self.copies = []
        width = target.shape[1] // parts
        for part in range(parts):
            cols = pl.ds(part * width, width)
            source = pl.ds(column + part * width, width)
            row = []
            for index, piece in enumerate(pieces):
                start = pl.multiple_of(offsets[first + index], 16)
                row.append(
                    pltpu.make_async_copy(
                        piece.at[:, source],
                        target.at[pl.ds(start, piece.shape[0]), cols],
                        sems.at[index, part],
                    )
                )
            self.copies.append(row)

    def start(self):
        for row in self.copies:
            for copy in row:
                copy.start()

    def wait(self, part):
        for copy in self.copies[part]:
            copy.wait()


def total_rows(pieces):
    return sum(piece.shape[0] for piece in pieces)


def project_kernel(count, column, groups, offs, h_ref, gain, shift, bias, down, up, *rest):
    pieces, rest = rest[:count], rest[count:]
    outs, (u_ref, a_ref), (weight, sems) = rest[:groups], rest[groups : groups + 2], rest[groups + 2 :]
    parts = 3 * groups
    loads = Loads(pieces, column, offs, 1, weight, sems, parts)
    loads.start()
    member = offs[0]
    model = h_ref.shape[1]
    width = model // groups
    unit, _ = normalise(h_ref[...].astype(full))
    a = (unit * gain[...] + shift[...]).astype(low)
    a_ref[...] = a
    u = dot(a, down[...]).astype(low)
    u_ref[...] = u
    for part in range(parts):
        kind, group = part // groups, part % groups
        loads.wait(part)
        cols = pl.ds(part * width, width)
        value = dot(a, weight[:, cols])
        if kind != 1:
            at = pl.ds((kind // 2) * model + group * width, width)
            value = value + bias[:, at] + dot(u, up[:, at])
        value = value.astype(low)
        for step in range(groups):

            @pl.when(member == (group ^ step))
            def _():
                outs[step][:, pl.ds(kind * width, width)] = value


def project(offs, hidden, gain, shift, bias, down, up, pieces, groups):
    tokens, model = hidden.shape
    width = 3 * model // groups
    outs = [jax.ShapeDtypeStruct((tokens, width), low)] * groups
    outs += [jax.ShapeDtypeStruct((tokens, LANES), low), jax.ShapeDtypeStruct((tokens, model), low)]
    pieces, column = pieces
    count = len(pieces)
    flops = 2 * tokens * model * 3 * model
    result = pl.pallas_call(
        functools.partial(project_kernel, count, column, groups),
        out_shape=outs,
        in_specs=[smem()] + [vmem()] * 6 + [hbm()] * count,
        out_specs=[vmem()] * len(outs),
        scratch_shapes=[
            pltpu.VMEM((model, 3 * model), low),
            pltpu.SemaphoreType.DMA((count, 3 * groups)),
        ],
        compiler_params=params(),
        cost_estimate=pl.CostEstimate(
            flops=flops, bytes_accessed=2 * model * 3 * model + 10 * tokens * model, transcendentals=0
        ),
        name="project",
    )(offs, hidden, gain, shift, bias, down, up, *pieces)
    return result[:groups], result[groups], result[groups + 1]


def attend_kernel(groups, offs, *rest):
    pieces, rest = rest[:groups], rest[groups:]
    outs, (o_ref, lse_ref), (qkv, lse_cols, sems) = rest[:groups], rest[groups : groups + 2], rest[groups + 2 :]
    member = offs[0]
    count, width3 = pieces[0].shape
    width = width3 // 3
    length = count * groups
    pairs = width // LANES
    block = 256
    loads = []
    for step in range(groups):
        rows = pl.ds(pl.multiple_of((member ^ step) * count, count), count)
        copy = pltpu.make_async_copy(pieces[step], qkv.at[rows, :], sems.at[step])
        copy.start()
        loads.append(copy)
    for copy in loads:
        copy.wait()
    lane = lax.broadcasted_iota(jnp.int32, (1, LANES), 1)
    keep = [(lane < HEAD).astype(low), (lane >= HEAD).astype(low)]
    causal = lax.broadcasted_iota(jnp.int32, (block, block), 1) <= lax.broadcasted_iota(
        jnp.int32, (block, block), 0
    )
    lse_cols[...] = jnp.zeros_like(lse_cols)

    @pl.loop(0, pairs)
    def _(pair):
        at = pl.multiple_of(pair * LANES, LANES)
        for start in range(0, length, block):
            rows = pl.ds(start, block)
            q = qkv[rows, pl.ds(at, LANES)]
            k = qkv[pl.ds(0, start + block), pl.ds(width + at, LANES)]
            v = qkv[pl.ds(0, start + block), pl.ds(2 * width + at, LANES)]
            mixed = jnp.zeros((block, LANES), full)
            logs = lse_cols[rows, :]
            for head in range(2):
                scores = dot_nt(q * (keep[head] * 0.125), k)
                corner = jnp.where(causal, scores[:, start:], -1e30)
                if start:
                    scores = jnp.concatenate([scores[:, :start], corner], axis=1)
                else:
                    scores = corner
                top = jnp.max(scores, axis=1, keepdims=True)
                weights = jnp.exp(scores - top)
                total = jnp.sum(weights, axis=1, keepdims=True)
                part = dot(weights.astype(low), v * keep[head])
                mixed = mixed + part * (1.0 / total)
                logs = jnp.where(lane == 2 * pair + head, top + jnp.log(total), logs)
            lse_cols[rows, :] = logs
            o_ref[rows, pl.ds(at, LANES)] = mixed.astype(low)

    lse_ref[...] = lse_cols[...].T
    for step in range(groups):
        rows = pl.ds(pl.multiple_of((member ^ step) * count, count), count)
        outs[step][...] = o_ref[rows, :]


def attend(offs, pieces):
    groups = len(pieces)
    count, width3 = pieces[0].shape
    width, length = width3 // 3, count * groups
    outs = [jax.ShapeDtypeStruct((count, width), low)] * groups
    outs += [jax.ShapeDtypeStruct((length, width), low), jax.ShapeDtypeStruct((LANES, length), full)]
    result = pl.pallas_call(
        functools.partial(attend_kernel, groups),
        out_shape=outs,
        in_specs=[smem()] + [hbm()] * groups,
        out_specs=[vmem()] * len(outs),
        scratch_shapes=[
            pltpu.VMEM((length, width3), low),
            pltpu.VMEM((length, LANES), full),
            pltpu.SemaphoreType.DMA((groups,)),
        ],
        compiler_params=params(),
        cost_estimate=pl.CostEstimate(
            flops=8 * length * length * width, bytes_accessed=10 * length * width, transcendentals=length * length * width // HEAD
        ),
        name="attend",
    )(offs, *pieces)
    return result[:groups], result[groups], result[groups + 1]


def attend_back_kernel(groups, offs, *rest):
    pieces, grads, rest = rest[:groups], rest[groups : 2 * groups], rest[2 * groups :]
    (o_ref, lse_ref), rest = rest[:2], rest[2:]
    outs, (qkv, d_out, result, inner, sems) = rest[:groups], rest[groups:]
    member = offs[0]
    count, width3 = pieces[0].shape
    width = width3 // 3
    length = count * groups
    pairs = width // LANES
    block = 256
    loads = []
    for step in range(groups):
        rows = pl.ds(pl.multiple_of((member ^ step) * count, count), count)
        for kind, (source, target) in enumerate(((pieces[step], qkv), (grads[step], d_out))):
            copy = pltpu.make_async_copy(source, target.at[rows, :], sems.at[kind, step])
            copy.start()
            loads.append(copy)
    for copy in loads:
        copy.wait()
    lane = lax.broadcasted_iota(jnp.int32, (1, LANES), 1)
    keep = [(lane < HEAD).astype(low), (lane >= HEAD).astype(low)]
    causal = lax.broadcasted_iota(jnp.int32, (block, block), 0) <= lax.broadcasted_iota(
        jnp.int32, (block, block), 1
    )
    heads = width // HEAD
    of_head = (
        lax.broadcasted_iota(jnp.int32, (max(heads, 8), width), 1) // HEAD
        == lax.broadcasted_iota(jnp.int32, (max(heads, 8), width), 0)
    ).astype(low)
    product = d_out[...].astype(full) * o_ref[...].astype(full)
    high = product.astype(low)
    rest_of = (product - high.astype(full)).astype(low)
    inner[...] = dot_nt(of_head, high) + dot_nt(of_head, rest_of)

    @pl.loop(0, pairs)
    def _(pair):
        at = pl.multiple_of(pair * LANES, LANES)
        grad_k = jnp.zeros((length, LANES), full)
        grad_v = jnp.zeros((length, LANES), full)
        for start in reversed(range(0, length, block)):
            rows = pl.ds(start, block)
            upto = start + block
            q = qkv[rows, pl.ds(at, LANES)]
            d = d_out[rows, pl.ds(at, LANES)]
            k = qkv[pl.ds(0, upto), pl.ds(width + at, LANES)]
            v = qkv[pl.ds(0, upto), pl.ds(2 * width + at, LANES)]
            grad_q = jnp.zeros((block, LANES), full)
            for head in range(2):
                q_head = q * (keep[head] * 0.125)
                d_head = d * keep[head]
                scores = dot_nt(k, q_head)
                log_sum = lse_ref[pl.ds(2 * pair + head, 1), rows]
                probs = jnp.exp(scores - log_sum)
                corner = jnp.where(causal, probs[start:], 0.0)
                probs = jnp.concatenate([probs[:start], corner], axis=0) if start else corner
                d_probs = dot_nt(v, d_head)
                d_scores = (probs * (d_probs - inner[pl.ds(2 * pair + head, 1), rows])).astype(low)
                more_v = dot(probs.astype(low), d_head)
                more_k = dot(d_scores, q_head)
                if upto < length:
                    zeros = jnp.zeros((length - upto, LANES), full)
                    more_v = jnp.concatenate([more_v, zeros], axis=0)
                    more_k = jnp.concatenate([more_k, zeros], axis=0)
                grad_v = grad_v + more_v
                grad_k = grad_k + more_k
                grad_q = grad_q + dot_tn(d_scores, k * (keep[head] * 0.125))
            result[rows, pl.ds(at, LANES)] = grad_q.astype(low)
        result[:, pl.ds(width + at, LANES)] = grad_k.astype(low)
        result[:, pl.ds(2 * width + at, LANES)] = grad_v.astype(low)

    for step in range(groups):
        rows = pl.ds(pl.multiple_of((member ^ step) * count, count), count)
        outs[step][...] = result[rows, :]


def attend_back(offs, pieces, grads, mixed, lse):
    groups = len(pieces)
    count, width3 = pieces[0].shape
    width, length = width3 // 3, count * groups
    outs = [jax.ShapeDtypeStruct((count, width3), low)] * groups
    return pl.pallas_call(
        functools.partial(attend_back_kernel, groups),
        out_shape=outs,
        in_specs=[smem()] + [hbm()] * (2 * groups) + [vmem()] * 2,
        out_specs=[vmem()] * len(outs),
        scratch_shapes=[
            pltpu.VMEM((length, width3), low),
            pltpu.VMEM((length, width), low),
            pltpu.VMEM((length, width3), low),
            pltpu.VMEM((max(width // HEAD, 8), length), full),
            pltpu.SemaphoreType.DMA((2, groups)),
        ],
        compiler_params=params(),
        cost_estimate=pl.CostEstimate(
            flops=20 * length * length * width, bytes_accessed=16 * length * width, transcendentals=length * length * width // HEAD
        ),
        name="attend_back",
    )(offs, *pieces, *grads, mixed, lse)


def mix_kernel(count, column, groups, offs, h_ref, bias, gain, shift, *rest):
    mixed, pieces, rest = rest[:groups], rest[groups : groups + count], rest[groups + count :]
    m_ref, c_ref, weight, sems = rest
    loads = Loads(pieces, column, offs, 1, weight, sems, 1)
    loads.start()
    loads.wait(0)
    width = mixed[0].shape[1]
    total = h_ref[...].astype(full) + bias[...]
    for step in range(groups):
        rows = pl.ds(pl.multiple_of((offs[0] ^ step) * width, width), width)
        total = total + dot(mixed[step][...], weight[rows, :])
    m_ref[...] = total
    unit, _ = normalise(total)
    c_ref[...] = (unit * gain[...] + shift[...]).astype(low)


def mix(offs, hidden, bias, gain, shift, mixed, pieces):
    pieces, column = pieces
    groups, count = len(mixed), len(pieces)
    tokens, model = hidden.shape
    return pl.pallas_call(
        functools.partial(mix_kernel, count, column, groups),
        out_shape=[jax.ShapeDtypeStruct((tokens, model), full), jax.ShapeDtypeStruct((tokens, model), low)],
        in_specs=[smem()] + [vmem()] * (4 + groups) + [hbm()] * count,
        out_specs=[vmem()] * 2,
        scratch_shapes=[pltpu.VMEM((model, model), low), pltpu.SemaphoreType.DMA((count, 1))],
        compiler_params=params(),
        cost_estimate=pl.CostEstimate(
            flops=2 * tokens * model * model, bytes_accessed=2 * model * model + 12 * tokens * model, transcendentals=0
        ),
        name="mix",
    )(offs, hidden, bias, gain, shift, *mixed, *pieces)


ROOT = 0.7978845608028654
CUBE = 0.044715


def feed_kernel(ups, downs, columns, parts, offs, c_ref, m_ref, up_bias, down_bias, *rest):
    up_pieces, down_pieces, rest = rest[:ups], rest[ups : ups + downs], rest[ups + downs :]
    h_ref, low_ref, slope_ref, up, down, acted, up_sems, down_sems = rest
    up_loads = Loads(up_pieces, columns[0], offs, 0, up, up_sems, parts)
    down_loads = Loads(down_pieces, columns[1], offs, ups, down, down_sems, 1)
    up_loads.start()
    down_loads.start()
    width = up.shape[1] // parts
    c = c_ref[...]
    for part in range(parts):
        cols = pl.ds(part * width, width)
        up_loads.wait(part)
        z = dot(c, up[:, cols]) + up_bias[:, cols]
        square = z * z
        t = jnp.tanh(ROOT * z * (1.0 + CUBE * square))
        half = 0.5 * (1.0 + t)
        acted[:, cols] = (z * half).astype(low)
        slope_ref[:, cols] = (
            half + z * (0.5 * ROOT) * (1.0 - t * t) * (1.0 + 3.0 * CUBE * square)
        ).astype(low)
    down_loads.wait(0)
    model = c_ref.shape[1]
    step = 256
    for start in range(0, model, step):
        cols = pl.ds(start, step)
        after = m_ref[:, cols] + (dot(acted[...], down[:, cols]) + down_bias[:, cols])
        h_ref[:, cols] = after
        low_ref[:, cols] = after.astype(low)


def feed(offs, second, middle, up_bias, down_bias, up_pieces, down_pieces):
    tokens, model = middle.shape
    hidden = up_bias.shape[1]
    (up_pieces, up_column), (down_pieces, down_column) = up_pieces, down_pieces
    ups, downs = len(up_pieces), len(down_pieces)
    parts = 8
    return pl.pallas_call(
        functools.partial(feed_kernel, ups, downs, (up_column, down_column), parts),
        out_shape=[
            jax.ShapeDtypeStruct((tokens, model), full),
            jax.ShapeDtypeStruct((tokens, model), low),
            jax.ShapeDtypeStruct((tokens, hidden), low),
        ],
        in_specs=[smem()] + [vmem()] * 4 + [hbm()] * (ups + downs),
        out_specs=[vmem()] * 3,
        scratch_shapes=[
            pltpu.VMEM((model, hidden), low),
            pltpu.VMEM((hidden, model), low),
            pltpu.VMEM((tokens, hidden), low),
            pltpu.SemaphoreType.DMA((ups, parts)),
            pltpu.SemaphoreType.DMA((downs, 1)),
        ],
        compiler_params=params(),
        cost_estimate=pl.CostEstimate(
            flops=4 * tokens * model * hidden, bytes_accessed=4 * model * hidden + 4 * tokens * hidden, transcendentals=tokens * hidden
        ),
        name="feed",
    )(offs, second, middle, up_bias, down_bias, *up_pieces, *down_pieces)


def feed_back_kernel(ups, downs, outs_count, columns, groups, parts, offs, g_ref, m_ref, slope_ref, gain, *rest):
    up_pieces, rest = rest[:ups], rest[ups:]
    down_pieces, rest = rest[:downs], rest[downs:]
    out_pieces, rest = rest[:outs_count], rest[outs_count:]
    mid_ref, rest = rest[0], rest[1:]
    outs, rest = rest[:groups], rest[groups:]
    up, down, out, d_pre, d_second, up_sems, down_sems, out_sems = rest
    down_loads = Loads(down_pieces, columns[1], offs, 1 + ups, down, down_sems, 1)
    up_loads = Loads(up_pieces, columns[0], offs, 1, up, up_sems, 1)
    out_loads = Loads(out_pieces, columns[2], offs, 1 + ups + downs, out, out_sems, 1)
    down_loads.start()
    up_loads.start()
    out_loads.start()
    hidden = down.shape[0]
    model = up.shape[0]
    width = hidden // parts
    g = g_ref[...].astype(low)
    down_loads.wait(0)
    for part in range(parts):
        cols = pl.ds(part * width, width)
        d_acted = dot_nt(g, down[cols, :])
        d_pre[:, cols] = (d_acted * slope_ref[:, cols].astype(full)).astype(low)
    up_loads.wait(0)
    step = 256
    for start in range(0, model, step):
        cols = pl.ds(start, step)
        d_second[:, cols] = dot_nt(d_pre[...], up[cols, :])
    unit, scale = normalise(m_ref[...])
    grad = g_ref[...].astype(full) + norm_back(unit, scale, gain[...], d_second[...])
    mid_ref[...] = grad
    grad = grad.astype(low)
    out_loads.wait(0)
    width = model // groups
    for group in range(groups):
        value = dot_nt(grad, out[pl.ds(group * width, width), :]).astype(low)
        for step in range(groups):

            @pl.when(offs[0] == (group ^ step))
            def _():
                outs[step][...] = value


def feed_back(offs, grad, middle, slope, gain, up_pieces, down_pieces, out_pieces, groups):
    tokens, model = middle.shape
    hidden = slope.shape[1]
    (up_pieces, up_column), (down_pieces, down_column) = up_pieces, down_pieces
    out_pieces, out_column = out_pieces
    columns = (up_column, down_column, out_column)
    ups, downs, outs_count = len(up_pieces), len(down_pieces), len(out_pieces)
    parts = 8
    result = pl.pallas_call(
        functools.partial(feed_back_kernel, ups, downs, outs_count, columns, groups, parts),
        out_shape=[jax.ShapeDtypeStruct((tokens, model), full)]
        + [jax.ShapeDtypeStruct((tokens, model // groups), low)] * groups,
        in_specs=[smem()] + [vmem()] * 4 + [hbm()] * (ups + downs + outs_count),
        out_specs=[vmem()] * (1 + groups),
        scratch_shapes=[
            pltpu.VMEM((model, hidden), low),
            pltpu.VMEM((hidden, model), low),
            pltpu.VMEM((model, model), low),
            pltpu.VMEM((tokens, hidden), low),
            pltpu.VMEM((tokens, model), full),
            pltpu.SemaphoreType.DMA((ups, 1)),
            pltpu.SemaphoreType.DMA((downs, 1)),
            pltpu.SemaphoreType.DMA((outs_count, 1)),
        ],
        compiler_params=params(),
        cost_estimate=pl.CostEstimate(
            flops=4 * tokens * model * hidden + 2 * tokens * model * model,
            bytes_accessed=4 * model * hidden + 4 * tokens * hidden,
            transcendentals=0,
        ),
        name="feed_back",
    )(offs, grad, middle, slope, gain, *up_pieces, *down_pieces, *out_pieces)
    return result[0], result[1:]


def project_back_kernel(count, column, groups, offs, mid_ref, h_ref, gain, a_ref, u_ref, down, up, *rest):
    grads, pieces, rest = rest[:groups], rest[groups : groups + count], rest[groups + count :]
    g_ref, low_ref, grad_a, grad_b, weight, d_all, d_normed, sems = rest
    loads = Loads(pieces, column, offs, 1, weight, sems, 1)
    loads.start()
    model = h_ref.shape[1]
    width = model // groups
    for step in range(groups):
        for kind in range(3):
            at = pl.multiple_of(kind * model + (offs[0] ^ step) * width, width)
            d_all[:, pl.ds(at, width)] = grads[step][:, pl.ds(kind * width, width)]
    d_query = d_all[:, pl.ds(0, model)]
    d_value = d_all[:, pl.ds(2 * model, model)]
    u = u_ref[...]
    lane = lax.broadcasted_iota(jnp.int32, (1, LANES), 1)
    half = 4
    u_query = jnp.where(lane < half, u, 0).astype(low)
    u_value = jnp.where(lane >= half, u, 0).astype(low)
    by_rank = dot_tn(u_query, d_query) + dot_tn(u_value, d_value)
    grad_b[...] = adapter_scale * by_rank[:8]
    d_inner = (
        dot_nt(d_query, up[:, pl.ds(0, model)]) + dot_nt(d_value, up[:, pl.ds(model, model)])
    ).astype(low)
    grad_a[...] = dot_tn(d_inner, a_ref[...])[:8]
    loads.wait(0)
    step = 256
    for start in range(0, model, step):
        rows = pl.ds(start, step)
        d_normed[:, rows] = dot_nt(d_all[...], weight[rows, :]) + dot_nt(d_inner, down[rows, :])
    unit, scale = normalise(h_ref[...].astype(full))
    grad = mid_ref[...] + norm_back(unit, scale, gain[...], d_normed[...])
    g_ref[...] = grad
    low_ref[...] = grad.astype(low)


def project_back(offs, mid, hidden, gain, normed, inner, down, up, grads, pieces):
    pieces, column = pieces
    groups, count = len(grads), len(pieces)
    tokens, model = hidden.shape
    return pl.pallas_call(
        functools.partial(project_back_kernel, count, column, groups),
        out_shape=[
            jax.ShapeDtypeStruct((tokens, model), full),
            jax.ShapeDtypeStruct((tokens, model), low),
            jax.ShapeDtypeStruct((8, model), full),
            jax.ShapeDtypeStruct((8, model), full),
        ],
        in_specs=[smem()] + [vmem()] * (7 + groups) + [hbm()] * count,
        out_specs=[vmem()] * 4,
        scratch_shapes=[
            pltpu.VMEM((model, 3 * model), low),
            pltpu.VMEM((tokens, 3 * model), low),
            pltpu.VMEM((tokens, model), full),
            pltpu.SemaphoreType.DMA((count, 1)),
        ],
        compiler_params=params(),
        cost_estimate=pl.CostEstimate(
            flops=2 * tokens * model * 3 * model, bytes_accessed=6 * model * model + 24 * tokens * model, transcendentals=0
        ),
        name="project_back",
    )(offs, mid, hidden, gain, normed, inner, down, up, *grads, *pieces)

def reshard_perms(sp_size, dp_size):
    quarter = sp_size // 4
    perms = []
    for part in range(2):
        perm = []
        for s in range(sp_size):
            for d in range(dp_size):
                doc = 2 * (d & 1) + ((s & 1) ^ part)
                member = s >> 1
                target_sp = doc * quarter + (member >> 1)
                target_dp = 2 * (d >> 1) + (member & 1)
                perm.append((s * dp_size + d, target_sp * dp_size + target_dp))
        perms.append(perm)
    return perms


def member_perm(sp_size, dp_size, step):
    quarter = sp_size // 4
    perm = []
    for s in range(sp_size):
        for d in range(dp_size):
            doc, high = s // quarter, s % quarter
            member = (2 * high + (d & 1)) ^ step
            target_sp = doc * quarter + (member >> 1)
            target_dp = 2 * (d >> 1) + (member & 1)
            perm.append((s * dp_size + d, target_sp * dp_size + target_dp))
    return perm


class Plan:
    def __init__(self, sp_size, dp_size):
        self.sp_size, self.dp_size = sp_size, dp_size
        self.members = sp_size // 2
        self.perms = reshard_perms(sp_size, dp_size)
        self.back = [[(b, a) for a, b in perm] for perm in self.perms]
        self.s = lax.axis_index("sp")
        self.d = lax.axis_index("dp")
        quarter = sp_size // 4
        self.doc = self.s // quarter
        self.member = 2 * (self.s % quarter) + (self.d & 1)

    def gather_doc(self, blocks):
        odd = self.s & 1
        got = []
        for part in range(2):
            block = lax.dynamic_index_in_dim(blocks, odd ^ part, 0, keepdims=False)
            got.append(lax.ppermute(block, ("sp", "dp"), self.perms[part]))
        flip = (self.doc & 1) == 1
        first = jnp.where(flip, got[1], got[0])
        second = jnp.where(flip, got[0], got[1])
        return jnp.concatenate([first, second], axis=0)

    def scatter_doc(self, rows):
        half = rows.shape[0] // 2
        blocks = rows.reshape(2, half, rows.shape[1])
        got = []
        for part in range(2):
            block = lax.dynamic_index_in_dim(blocks, (self.doc & 1) ^ part, 0, keepdims=False)
            got.append(lax.ppermute(block, ("sp", "dp"), self.back[part]))
        flip = (self.s & 1) == 1
        first = jnp.where(flip, got[1], got[0])
        second = jnp.where(flip, got[0], got[1])
        return jnp.stack([first, second])

    def swap(self, parts):
        out = [parts[0]]
        for step in range(1, self.members):
            perm = member_perm(self.sp_size, self.dp_size, step)
            out.append(lax.ppermute(parts[step], ("sp", "dp"), perm))
        return out


def all_sum(value, sp_size, dp_size):
    total = sp_size * dp_size
    step = 1
    while step < total:
        value = value + lax.ppermute(
            value, ("sp", "dp"), [(i, i ^ step) for i in range(total)]
        )
        step *= 2
    return value


def fetch(plan, shard):
    if plan.sp_size != 4:
        return [lax.all_gather(shard, ("sp", "dp"), axis=0, tiled=True)], [0]
    block = lax.all_gather(shard, "dp", axis=0, tiled=True)
    rows = block.shape[0]
    half, quarter = rows // 2, rows // 4
    s, core = plan.s, plan.d & 1
    mine = lax.dynamic_slice_in_dim(block, core * half, half, axis=0)
    over_x = [(i, i ^ 1) for i in range(4)]
    over_y = [(i, i ^ 2) for i in range(4)]
    over_core = [(i, i ^ 1) for i in range(plan.dp_size)]
    from_x = lax.ppermute(mine, "sp", over_x)
    from_y = lax.ppermute(mine, "sp", over_y)
    far_first = lax.ppermute(from_y[:quarter], "sp", over_x)
    far_second = lax.ppermute(from_x[quarter:], "sp", over_y)
    got = [from_x, from_y, far_first, far_second]
    got += [lax.ppermute(piece, "dp", over_core) for piece in got]
    starts = []
    for near in (core, 1 - core):
        base = near * half
        starts += [(s ^ 1) * rows + base, (s ^ 2) * rows + base]
        starts += [(s ^ 3) * rows + base, (s ^ 3) * rows + base + quarter]
    return [block] + got, [s * rows] + starts


def on_device(
    tokens,
    cotangent,
    layer_norm_gain,
    layer_norm_bias,
    query_key_value_weight,
    query_value_bias,
    attention_out_weight,
    output_projection_bias,
    feed_up_weight,
    feed_up_bias,
    feed_down_weight,
    adapter_down_maps,
    adapter_up_weights,
):
    layers = query_key_value_weight.shape[0]
    model = tokens.shape[2]
    rank = adapter_down_maps.shape[3]
    plan = Plan(lax.axis_size("sp"), lax.axis_size("dp"))
    groups = plan.members
    member = plan.member.astype(jnp.int32)

    def table(*entries):
        return jnp.stack([jnp.asarray(entry, jnp.int32) for entry in entries])

    weights = []
    for layer in range(layers):
        if layer == 0:
            joined = [
                query_key_value_weight[layer],
                jnp.concatenate([attention_out_weight[layer], feed_up_weight[layer]], axis=1),
            ]
        else:
            joined = [
                jnp.concatenate(
                    [query_key_value_weight[layer], attention_out_weight[layer], feed_up_weight[layer]],
                    axis=1,
                )
            ]
        got = [fetch(plan, shard) for shard in joined]
        down, starts_down = fetch(plan, feed_down_weight[layer])
        starts = got[0][1]
        if layer == 0:
            qkv, out, up = (got[0][0], 0), (got[1][0], 0), (got[1][0], model)
        else:
            qkv, out, up = (got[0][0], 0), (got[0][0], 3 * model), (got[0][0], 4 * model)
        weights.append((qkv, out, up, (down, 0), starts, starts_down))

    adapters = []
    for layer in range(layers):
        down = jnp.concatenate([adapter_down_maps[layer, 0], adapter_down_maps[layer, 1]], axis=1)
        down = jnp.pad(down, ((0, 0), (0, LANES - 2 * rank)))
        up = adapter_up_weights[layer] * jnp.asarray(adapter_scale, low)
        up = jnp.concatenate(
            [
                jnp.pad(up[0], ((0, LANES - rank), (0, 0))),
                jnp.pad(up[1], ((rank, LANES - 2 * rank), (0, 0))),
            ],
            axis=1,
        )
        adapters.append((down, up))

    hidden = plan.gather_doc(tokens)
    grad = plan.gather_doc(cotangent)
    saved, outputs = [], []
    for layer in range(layers):
        qkv_w, out_w, up_w, down_w, starts, starts_down = weights[layer]
        gain, shift = layer_norm_gain[layer], layer_norm_bias[layer]
        down, up = adapters[layer]
        offs = table(member, *starts)
        bias = query_value_bias[layer].reshape(1, 2 * model)
        parts, inner, normed = project(
            offs, hidden, gain[:1], shift[:1], bias, down, up, qkv_w, groups
        )
        parts = plan.swap(parts)
        mixed_parts, mixed, lse = attend(offs, parts)
        mixed_parts = plan.swap(mixed_parts)
        middle, second = mix(
            offs, hidden, output_projection_bias[layer, :1], gain[1:], shift[1:], mixed_parts, out_w
        )
        after, after_low, slope = feed(
            table(*starts, *starts_down),
            second,
            middle,
            feed_up_bias[layer : layer + 1],
            output_projection_bias[layer, 1:],
            up_w,
            down_w,
        )
        saved.append((hidden, normed, inner, parts, mixed, lse, middle, slope))
        outputs.append(plan.scatter_doc(after_low).astype(full))
        hidden = after
    sums = [None] * layers
    for layer in reversed(range(layers)):
        qkv_w, out_w, up_w, down_w, starts, starts_down = weights[layer]
        hidden, normed, inner, parts, mixed, lse, middle, slope = saved[layer]
        gain = layer_norm_gain[layer]
        down, up = adapters[layer]
        offs = table(member, *starts)
        mid, d_mixed = feed_back(
            table(member, *starts, *starts_down, *starts),
            grad,
            middle,
            slope,
            gain[1:],
            up_w,
            down_w,
            out_w,
            groups,
        )
        d_mixed = plan.swap(d_mixed)
        grads = plan.swap(attend_back(offs, parts, d_mixed, mixed, lse))
        grad, grad_low, grad_a, grad_b = project_back(
            offs, mid, hidden, gain[:1], normed, inner, down, up, grads, qkv_w
        )
        sums[layer] = all_sum(jnp.concatenate([grad_a, grad_b]), plan.sp_size, plan.dp_size)
    total = jnp.stack(sums).reshape(layers, 2, 8, model)[:, :, : 2 * rank]
    total = total.reshape(layers, 2, 2, rank, model)
    grad_tokens = plan.scatter_doc(grad_low).astype(full)
    return (jnp.stack(outputs), grad_tokens, total[:, 0].swapaxes(-1, -2), total[:, 1])


def solution(mesh):
    in_specs = (
        P("dp", "sp", None),
        P("dp", "sp", None),
        P(),
        P(),
        P(None, ("sp", "dp"), None),
        P(),
        P(None, ("sp", "dp"), None),
        P(),
        P(None, ("sp", "dp"), None),
        P(),
        P(None, ("sp", "dp"), None),
        P(),
        P(),
    )
    out_specs = (P(None, "dp", "sp", None), P("dp", "sp", None), P(), P())
    return jax.shard_map(
        on_device, mesh=mesh, in_specs=in_specs, out_specs=out_specs, check_vma=False
    )
```

time: 1110 us -> 605 us (0.55)
  matrix products: 282 us -> 0 us
  waiting for transfers between devices: 500 us -> 239 us
  Pallas kernels: 0 us -> 228 us
  local copies, waits for them, and re-layouts: 153 us -> 43.8 us
  other arithmetic: 83.8 us -> 12.7 us
    dot_general x82 -> x0, matrix products: 282 us -> none  [the longest x8 39.4 us: attend_back(): jnp.einsum('nqhe,nkhe->nhqk', d_block, v_doc, preferred_element_type=jnp....]
    pallas_call x0 -> x14, Pallas kernels: none -> 228 us  [the longest x2 46.3 us: feed_back(): pl.pallas_call(functools.partial(feed_back_kernel, ups, downs, outs_count...]
    all_gather x8 -> x5, waiting for transfers between devices: 271 us -> 50.7 us  [fetch(): block = lax.all_gather(shard, 'dp', axis=0, tiled=True)]
    ppermute x0 -> x68, waiting for transfers between devices: none -> 188 us  [the longest x5 94.9 us: fetch(): far_first = lax.ppermute(from_y[:quarter], 'sp', over_x)]
    psum x1 -> x0, waiting for transfers between devices: 117 us -> none  [on_device(): lax.psum((jnp.stack(grads_a[::-1]), jnp.stack(grads_b[::-1])), ('sp', 'dp'))]
    all_to_all x16 -> x0, waiting for transfers between devices: 110 us -> none  [the longest x2 37.2 us: on_device(): lax.all_to_all(mixed, 'sp', split_axis=1, concat_axis=2, tiled=True)]
    all_to_all x16 -> x0, starting transfers between devices: 66.1 us -> none  [the longest x2 8.9 us: on_device(): lax.all_to_all(grad_v, 'sp', split_axis=1, concat_axis=2, tiled=True)]
    ppermute x0 -> x68, starting transfers between devices: none -> 59.5 us  [the longest x10 13.8 us: all_sum(): lax.ppermute(value, ('sp', 'dp'), [(i, i ^ step) for i in range(total)])]
  transfers between devices with their start and end apart: 25 -> 73, of which waited for: 19 -> 23; matrix products, arithmetic and copies ran while one was open for 29% -> 7% of each run, Pallas kernels for 0% -> 17%
where the time goes in v1:
time: 605 us; the launch traced here: 598 us
  waiting for transfers between devices  239 us (40%)
  Pallas kernels  228 us (38%)
  starting transfers between devices  59.7 us (10%)
  local copies, waits for them, and re-layouts  43.8 us (7%)
  between operations  14.9 us (2%)
  other arithmetic  12.7 us (2%)
    ppermute x5, waiting for transfers between devices, fetch(): far_first = lax.ppermute(from_y[:quarter], 'sp', over_x)  94.9 us
    all_gather x5, waiting for transfers between devices, fetch(): block = lax.all_gather(shard, 'dp', axis=0, tiled=True)  50.7 us
    ppermute x5, waiting for transfers between devices, fetch(): from_y = lax.ppermute(mine, 'sp', over_y)  47.5 us
    pallas_call x2, Pallas kernels, feed_back(): pl.pallas_call(functools.partial(feed_back_kernel, ups, downs, outs_count...  46.3 us
    pallas_call x2, Pallas kernels, attend_back(): pl.pallas_call(functools.partial(attend_back_kernel, groups), out_shape=o...  44.3 us
    pallas_call x2, Pallas kernels, feed(): pl.pallas_call(functools.partial(feed_kernel, ups, downs, (up_column, dow...  43 us
    pallas_call x2, Pallas kernels, attend(): pl.pallas_call(functools.partial(attend_kernel, groups), out_shape=outs,...  35.1 us
    pallas_call x2, Pallas kernels, project_back(): pl.pallas_call(functools.partial(project_back_kernel, count, column, grou...  25.5 us
  transfers between devices with their start and end apart: 73, of which 23 were waited for; matrix products, arithmetic and copies ran while one was open for 7% of the time, Pallas kernels for 17%

profile of v1, /device:TPU:0, one launch (start us, length us, event | category | flops | bytes accessed | tf_op | source)
XLA Modules:
  0.0 597.7 jit_solution(15734640102605740400)
XLA Ops:
  16.8 25.2 %all-gather.15.cloned.1.call-done = bf16[1,1024,1024]{2,1,0:T(8,128)(2,1)} async-done(((bf16[1,128,1024]{2,1,0:T(8,128)(2,1)}), bf16[1,1024,1024]{2,1,0:T(8,128)(2,1)}) %all-gather.15.cloned.1.call-update) | async-done | bytes 2097168 | tf_op jit(solution)/shard_map/all_gather | solution.py:650
  45.8 22.5 %all-gather.13.cloned.1.call-done = bf16[1,256,3072]{2,1,0:T(8,128)(2,1)} async-done(((bf16[1,32,3072]{2,1,0:T(8,128)(2,1)}), bf16[1,256,3072]{2,1,0:T(8,128)(2,1)}) %all-gather.13.cloned.1.call-update) | async-done | bytes 1572880 | tf_op jit(solution)/shard_map/all_gather | solution.py:650
  74.9 14.4 %collective-permute-done.3.rest_2_.rest_4_ = bf16[128,3072]{1,0:T(8,128)(2,1)} collective-permute-done((bf16[128,3072]{1,0:T(8,128)(2,1)S(1)}, bf16[128,3072]{1,0:T(8,128)(2,1)}, u32[]{:S(2)}, u32[]{:S(2)}) %collective-permute-start.3) | collective-permute-done | bytes 786464 | tf_op jit(solution)/shard_map/ppermute | solution.py:659
  89.3 5.4 collective-permute-start.1
  104.0 18.3 %collective-permute-done.4.rest_3_.rest_5_ = bf16[64,3072]{1,0:T(8,128)(2,1)S(1)} collective-permute-done((bf16[64,3072]{1,0:T(8,128)(2,1)S(1)}, bf16[64,3072]{1,0:T(8,128)(2,1)S(1)}, u32[]{:S(2)}, u32[]{:S(2)}) %collective-permute-start.4) | collective-permute-done | bytes 393248 | tf_op jit(solution)/shard_map/ppermute | solution.py:660
  126.7 5.9 collective-permute-done.22.rest_12_
  136.4 10.6 %project.2 = (bf16[512,1536]{1,0:T(8,128)(2,1)}, bf16[512,1536]{1,0:T(8,128)(2,1)}, bf16[512,128]{1,0:T(8,128)(2,1)}, bf16[512,1024]{1,0:T(8,128)(2,1)}) custom-call(s32[10]{0:T(128)} %stack.93.offs, bf16[512,1024]{1,0:T(8,128)(2,1)} %pad_maximum_fusion.h_ref, f32[1,1024]{1,0:T(1,128)} %get-tuple-element.137.gain, f32[1,1024]{1,0:T(1,128)} %get-tuple-element.133.shift, ...), custom_call_target="tpu_custom_call" | custom-call | flops 3221225472 | bytes 11534336 | tf_op jit(solution)/shard_map/project/pallas_call | solution.py:128
  149.4 3.0 all-gather.11.cloned.1.call-done.rest_0_.rest_2_.rest_18_
  152.4 3.1 constant_dynamic-slice_fusion
  157.0 12.1 %collective-permute-done.13.rest_4_.rest_2_.rest_20_ = bf16[128,5120]{1,0:T(8,128)(2,1)} collective-permute-done((bf16[128,5120]{1,0:T(8,128)(2,1)}, bf16[128,5120]{1,0:T(8,128)(2,1)}, u32[]{:S(2)}, u32[]{:S(2)}) %collective-permute-start.13) | collective-permute-done | bytes 1310752 | tf_op jit(solution)/shard_map/ppermute | solution.py:659
  171.7 7.5 %collective-permute-done.12.rest_3_.rest_1_.rest_19_ = bf16[128,5120]{1,0:T(8,128)(2,1)} collective-permute-done((bf16[128,5120]{1,0:T(8,128)(2,1)}, bf16[128,5120]{1,0:T(8,128)(2,1)}, u32[]{:S(2)}, u32[]{:S(2)}) %collective-permute-start.12) | collective-permute-done | bytes 1310752 | tf_op jit(solution)/shard_map/ppermute | solution.py:658
  184.2 53.4 %collective-permute-done.14.rest_5_.rest_3_.rest_21_ = bf16[64,5120]{1,0:T(8,128)(2,1)} collective-permute-done((bf16[64,5120]{1,0:T(8,128)(2,1)S(1)}, bf16[64,5120]{1,0:T(8,128)(2,1)}, u32[]{:S(2)}, u32[]{:S(2)}) %collective-permute-start.14) | collective-permute-done | bytes 655392 | tf_op jit(solution)/shard_map/ppermute | solution.py:660
  238.2 17.5 %attend.2 = (bf16[512,512]{1,0:T(8,128)(2,1)}, bf16[512,512]{1,0:T(8,128)(2,1)}, bf16[1024,512]{1,0:T(8,128)(2,1)}, f32[128,1024]{1,0:T(8,128)}) custom-call(s32[10]{0:T(128)} %stack.93.offs, bf16[512,1536]{1,0:T(8,128)(2,1)} %get-tuple-element.45.rest_0_, bf16[512,1536]{1,0:T(8,128)(2,1)} %collective-permute-done.10.rest_1_), custom_call_target="tpu_custom_call" | custom-call | flops 4294967296 | bytes 5242880 | tf_op jit(solution)/shard_map/attend/pallas_call | solution.py:208
  267.6 17.3 %collective-permute-done.32.rest_3_.rest_5_.rest_21_ = bf16[64,8192]{1,0:T(8,128)(2,1)S(1)} collective-permute-done((bf16[64,8192]{1,0:T(8,128)(2,1)}, bf16[64,8192]{1,0:T(8,128)(2,1)S(1)}, u32[]{:S(2)}, u32[]{:S(2)}) %collective-permute-start.32) | collective-permute-done | bytes 1048608 | tf_op jit(solution)/shard_map/ppermute | solution.py:660
  286.9 6.2 %mix.2 = (f32[512,1024]{1,0:T(8,128)}, bf16[512,1024]{1,0:T(8,128)(2,1)}) custom-call(s32[10]{0:T(128)} %stack.93.offs, bf16[512,1024]{1,0:T(8,128)(2,1)} %pad_maximum_fusion.h_ref, f32[1,1024]{1,0:T(1,128)} %get-tuple-element.126.bias, f32[1,1024]{1,0:T(1,128)} %get-tuple-element.138.gain, f32[1,1024]{1,0:T(1,128)} %get-tuple-element.134.shift, ...), custom_call_target="tpu_custom_call" | custom-call | flops 1073741824 | bytes 8388608 | tf_op jit(solution)/shard_map/mix/pallas_call | solution.py:347
  293.1 21.6 %feed.2 = (f32[512,1024]{1,0:T(8,128)}, bf16[512,1024]{1,0:T(8,128)(2,1)}, bf16[512,4096]{1,0:T(8,128)(2,1)}) custom-call(s32[18]{0:T(128)} %stack.91.offs, bf16[512,1024]{1,0:T(8,128)(2,1)} %get-tuple-element.49.c_ref, f32[512,1024]{1,0:T(8,128)} %get-tuple-element.50.m_ref, f32[1,4096]{1,0:T(1,128)} %get-tuple-element.117.up_bias, ...), custom_call_target="tpu_custom_call" | custom-call | flops 8589934592 | bytes 25165824 | tf_op jit(solution)/shard_map/feed/pallas_call | solution.py:401
  316.0 10.6 %project.3 = (bf16[512,1536]{1,0:T(8,128)(2,1)}, bf16[512,1536]{1,0:T(8,128)(2,1)}, bf16[512,128]{1,0:T(8,128)(2,1)}, bf16[512,1024]{1,0:T(8,128)(2,1)}) custom-call(s32[10]{0:T(128)} %stack.93.offs, f32[512,1024]{1,0:T(8,128)} %get-tuple-element.52.h_ref, f32[1,1024]{1,0:T(1,128)} %get-tuple-element.136.gain, f32[1,1024]{1,0:T(1,128)} %get-tuple-element.132.shift, ...), custom_call_target="tpu_custom_call" | custom-call | flops 3221225472 | bytes 11534336 | tf_op jit(solution)/shard_map/project/pallas_call | solution.py:128
  332.9 21.0 %collective-permute-done.41.rest_11_ = bf16[512,1024]{1,0:T(8,128)(2,1)S(1)} collective-permute-done((bf16[512,1024]{1,0:T(8,128)(2,1)S(1)}, bf16[512,1024]{1,0:T(8,128)(2,1)S(1)}, u32[]{:S(2)}, u32[]{:S(2)}) %collective-permute-start.41) | collective-permute-done | bytes 1048608 | tf_op jit(solution)/shard_map/ppermute | solution.py:659
  357.3 10.0 %collective-permute-done.50 = bf16[256,1024]{1,0:T(8,128)(2,1)S(1)} collective-permute-done((bf16[256,1024]{1,0:T(8,128)(2,1)S(1)}, bf16[256,1024]{1,0:T(8,128)(2,1)S(1)}, u32[]{:S(2)}, u32[]{:S(2)}) %collective-permute-start.50) | collective-permute-done | bytes 524320 | tf_op jit(solution)/shard_map/ppermute | solution.py:610
  368.1 17.6 %attend.3 = (bf16[512,512]{1,0:T(8,128)(2,1)}, bf16[512,512]{1,0:T(8,128)(2,1)}, bf16[1024,512]{1,0:T(8,128)(2,1)}, f32[128,1024]{1,0:T(8,128)}) custom-call(s32[10]{0:T(128)} %stack.93.offs, bf16[512,1536]{1,0:T(8,128)(2,1)} %get-tuple-element.53.rest_0_, bf16[512,1536]{1,0:T(8,128)(2,1)} %collective-permute-done.38.rest_1_), custom_call_target="tpu_custom_call" | custom-call | flops 4294967296 | bytes 5242880 | tf_op jit(solution)/shard_map/attend/pallas_call | solution.py:208
  390.7 6.4 %mix.3 = (f32[512,1024]{1,0:T(8,128)}, bf16[512,1024]{1,0:T(8,128)(2,1)}) custom-call(s32[10]{0:T(128)} %stack.93.offs, f32[512,1024]{1,0:T(8,128)} %get-tuple-element.52.h_ref, f32[1,1024]{1,0:T(1,128)} %get-tuple-element.127.bias, f32[1,1024]{1,0:T(1,128)} %get-tuple-element.139.gain, f32[1,1024]{1,0:T(1,128)} %get-tuple-element.135.shift, ...), custom_call_target="tpu_custom_call" | custom-call | flops 1073741824 | bytes 8388608 | tf_op jit(solution)/shard_map/mix/pallas_call | solution.py:347
  398.1 21.5 %feed.3 = (f32[512,1024]{1,0:T(8,128)}, bf16[512,1024]{1,0:T(8,128)(2,1)}, bf16[512,4096]{1,0:T(8,128)(2,1)}) custom-call(s32[18]{0:T(128)} %stack.91.offs, bf16[512,1024]{1,0:T(8,128)(2,1)} %get-tuple-element.57.c_ref, f32[512,1024]{1,0:T(8,128)} %get-tuple-element.58.m_ref, f32[1,4096]{1,0:T(1,128)} %get-tuple-element.116.up_bias, ...), custom_call_target="tpu_custom_call" | custom-call | flops 8589934592 | bytes 25165824 | tf_op jit(solution)/shard_map/feed/pallas_call | solution.py:401
  419.6 22.9 %feed_back.2 = (f32[512,1024]{1,0:T(8,128)}, bf16[512,512]{1,0:T(8,128)(2,1)}, bf16[512,512]{1,0:T(8,128)(2,1)}) custom-call(s32[28]{0:T(128)} %stack.102.offs, bf16[512,1024]{1,0:T(8,128)(2,1)} %pad_maximum_fusion.1.g_ref, f32[512,1024]{1,0:T(8,128)} %get-tuple-element.58.m_ref, bf16[512,4096]{1,0:T(8,128)(2,1)} %get-tuple-element.60.slope_ref, ...), custom_call_target="tpu_custom_call" | custom-call | flops 9663676416 | bytes 25165824 | tf_op jit(solution)/shard_map/feed_back/pallas_call | solution.py:475
  445.5 22.2 %attend_back.2 = (bf16[512,1536]{1,0:T(8,128)(2,1)}, bf16[512,1536]{1,0:T(8,128)(2,1)}) custom-call(s32[10]{0:T(128)} %stack.93.offs, bf16[512,1536]{1,0:T(8,128)(2,1)} %get-tuple-element.53.rest_0_, bf16[512,1536]{1,0:T(8,128)(2,1)} %collective-permute-done.38.rest_1_, bf16[512,512]{1,0:T(8,128)(2,1)} %get-tuple-element.64.rest_2_, ...), custom_call_target="tpu_custom_call" | custom-call | flops 10737418240 | bytes 8388608 | tf_op jit(solution)/shard_map/attend_back/pallas_call | solution.py:307
  467.9 3.5 collective-permute-done.53.rest_1_
  472.5 13.0 %project_back.2 = (f32[512,1024]{1,0:T(8,128)}, bf16[512,1024]{1,0:T(8,128)(2,1)}, f32[8,1024]{1,0:T(8,128)}, f32[8,1024]{1,0:T(8,128)}) custom-call(s32[10]{0:T(128)} %stack.93.offs, f32[512,1024]{1,0:T(8,128)} %get-tuple-element.61.mid_ref, f32[512,1024]{1,0:T(8,128)} %get-tuple-element.52.h_ref, f32[1,1024]{1,0:T(1,128)} %get-tuple-element.136.gain, ...), custom_call_target="tpu_custom_call" | custom-call | flops 3221225472 | bytes 18874368 | tf_op jit(solution)/shard_map/project_back/pallas_call | solution.py:541
  485.6 23.4 %feed_back.3 = (f32[512,1024]{1,0:T(8,128)}, bf16[512,512]{1,0:T(8,128)(2,1)}, bf16[512,512]{1,0:T(8,128)(2,1)}) custom-call(s32[28]{0:T(128)} %stack.102.offs, f32[512,1024]{1,0:T(8,128)} %get-tuple-element.70.g_ref, f32[512,1024]{1,0:T(8,128)} %get-tuple-element.50.m_ref, bf16[512,4096]{1,0:T(8,128)(2,1)} %get-tuple-element.71.slope_ref, ...), custom_call_target="tpu_custom_call" | custom-call | flops 9663676416 | bytes 25165824 | tf_op jit(solution)/shard_map/feed_back/pallas_call | solution.py:475
  512.0 22.1 %attend_back.3 = (bf16[512,1536]{1,0:T(8,128)(2,1)}, bf16[512,1536]{1,0:T(8,128)(2,1)}) custom-call(s32[10]{0:T(128)} %stack.93.offs, bf16[512,1536]{1,0:T(8,128)(2,1)} %get-tuple-element.45.rest_0_, bf16[512,1536]{1,0:T(8,128)(2,1)} %collective-permute-done.10.rest_1_, bf16[512,512]{1,0:T(8,128)(2,1)} %get-tuple-element.75.rest_2_, ...), custom_call_target="tpu_custom_call" | custom-call | flops 10737418240 | bytes 8388608 | tf_op jit(solution)/shard_map/attend_back/pallas_call | solution.py:307
  542.6 12.5 %project_back.3 = (f32[512,1024]{1,0:T(8,128)}, bf16[512,1024]{1,0:T(8,128)(2,1)}, f32[8,1024]{1,0:T(8,128)}, f32[8,1024]{1,0:T(8,128)}) custom-call(s32[10]{0:T(128)} %stack.93.offs, f32[512,1024]{1,0:T(8,128)} %get-tuple-element.72.mid_ref, bf16[512,1024]{1,0:T(8,128)(2,1)} %pad_maximum_fusion.h_ref, f32[1,1024]{1,0:T(1,128)} %get-tuple-element.137.gain, ...), custom_call_target="tpu_custom_call" | custom-call | flops 3221225472 | bytes 18874368 | tf_op jit(solution)/shard_map/project_back/pallas_call | solution.py:541
  562.5 4.0 collective-permute-done.65
  569.6 3.3 collective-permute-done.60
  577.0 7.1 %collective-permute-done.61 = f32[16,1024]{1,0:T(8,128)S(1)} collective-permute-done((f32[16,1024]{1,0:T(8,128)S(1)}, f32[16,1024]{1,0:T(8,128)S(1)}, u32[]{:S(2)}, u32[]{:S(2)}) %collective-permute-start.61) | collective-permute-done | bytes 65568 | tf_op jit(solution)/shard_map/ppermute | solution.py:640
  (287 shorter events, 117.8 us)
Async XLA Ops:
  7.2 34.8 %all-gather.15.cloned.1.call-start = ((), (), s32[]{:S(2)}) async-start(), calls=%async_computation.3 | async-start | bytes 2359296 | tf_op jit(solution)/shard_map/all_gather | solution.py:650
  9.2 59.1 %all-gather.13.cloned.1.call-start = ((), (), s32[]{:S(2)}) async-start(), calls=%async_computation.2 | async-start | bytes 1769472 | tf_op jit(solution)/shard_map/all_gather | solution.py:650
  11.0 121.7 %all-gather.9.cloned.1.call-start = ((), (), s32[]{:S(2)}) async-start(), calls=%async_computation | async-start | bytes 2949120 | tf_op jit(solution)/shard_map/all_gather | solution.py:650
  11.9 140.5 %all-gather.11.cloned.1.call-start = ((), (), s32[]{:S(2)}) async-start(), calls=%async_computation.1 | async-start | bytes 4718592 | tf_op jit(solution)/shard_map/all_gather | solution.py:650
  12.8 314.4 %all-gather.17.cloned.1.call-start = ((), (), s32[]{:S(2)}) async-start(), calls=%async_computation.4 | async-start | bytes 2359296 | tf_op jit(solution)/shard_map/all_gather | solution.py:650
  13.9 85.7 %collective-permute-start = (bf16[256,1024]{1,0:T(8,128)(2,1)}, bf16[256,1024]{1,0:T(8,128)(2,1)}, u32[]{:S(2)}, u32[]{:S(2)}) collective-permute-start(bf16[256,1024]{1,0:T(8,128)(2,1)} %get-tuple-element.104), channel_id=1, source_target_pairs={{0,8},{1,24},{2,10},{3,26},{4,12},{5,28},{6,14},{7,30},{8,0},{9,16... | collective-permute-start | bytes 1572872 | tf_op jit(solution)/shard_map/ppermute | solution.py:610
  44.3 52.9 %collective-permute-start.21 = (bf16[512,1024]{1,0:T(8,128)(2,1)}, bf16[512,1024]{1,0:T(8,128)(2,1)S(1)}, u32[]{:S(2)}, u32[]{:S(2)}) collective-permute-start(bf16[512,1024]{1,0:T(8,128)(2,1)} %dynamic-slice_bitcast_fusion.1), channel_id=1, source_target_pairs={{0,16},{8,24},{16,0},{24,8},{1,17},{9,25},{17,1},{25,9},{2,18},{10... | collective-permute-start | bytes 3145736 | tf_op jit(solution)/shard_map/ppermute | solution.py:659
  73.7 52.3 %collective-permute-start.20 = (bf16[512,1024]{1,0:T(8,128)(2,1)}, bf16[512,1024]{1,0:T(8,128)(2,1)S(1)}, u32[]{:S(2)}, u32[]{:S(2)}) collective-permute-start(bf16[512,1024]{1,0:T(8,128)(2,1)} %dynamic-slice_bitcast_fusion.1), channel_id=1, source_target_pairs={{0,8},{8,0},{16,24},{24,16},{1,9},{9,1},{17,25},{25,17},{2,10},{10... | collective-permute-start | bytes 3145736 | tf_op jit(solution)/shard_map/ppermute | solution.py:658
  97.2 28.9 %collective-permute-start.6 = (bf16[128,3072]{1,0:T(8,128)(2,1)}, bf16[128,3072]{1,0:T(8,128)(2,1)}, u32[]{:S(2)}, u32[]{:S(2)}) collective-permute-start(bf16[128,3072]{1,0:T(8,128)(2,1)} %collective-permute-done.2.rest_1_.rest_3_), channel_id=1, source_target_pairs={{0,1},{1,0},{2,3},{3,2},{4,5},{5,4},{6,7},{7,6},{8,9},{9,8},{10,11... | collective-permute-start | bytes 2359304 | tf_op jit(solution)/shard_map/ppermute | solution.py:663
  99.6 33.1 %collective-permute-start.22 = (bf16[256,1024]{1,0:T(8,128)(2,1)}, bf16[256,1024]{1,0:T(8,128)(2,1)}, u32[]{:S(2)}, u32[]{:S(2)}) collective-permute-start(bf16[256,1024]{1,0:T(8,128)(2,1)} %slice.244), channel_id=1, source_target_pairs={{0,8},{8,0},{16,24},{24,16},{1,9},{9,1},{17,25},{25,17},{2,10},{10... | collective-permute-start | bytes 1572872 | tf_op jit(solution)/shard_map/ppermute | solution.py:660
  135.1 34.0 %collective-permute-start.13 = (bf16[128,5120]{1,0:T(8,128)(2,1)}, bf16[128,5120]{1,0:T(8,128)(2,1)}, u32[]{:S(2)}, u32[]{:S(2)}) collective-permute-start(bf16[128,5120]{1,0:T(8,128)(2,1)} %constant_dynamic-slice_fusion.1), channel_id=1, source_target_pairs={{0,16},{8,24},{16,0},{24,8},{1,17},{9,25},{17,1},{25,9},{2,18},{10... | collective-permute-start | bytes 3932168 | tf_op jit(solution)/shard_map/ppermute | solution.py:659
  147.0 37.1 %collective-permute-start.10 = (bf16[512,1536]{1,0:T(8,128)(2,1)}, bf16[512,1536]{1,0:T(8,128)(2,1)}, u32[]{:S(2)}, u32[]{:S(2)}) collective-permute-start(bf16[512,1536]{1,0:T(8,128)(2,1)} %get-tuple-element.46), channel_id=1, source_target_pairs={{0,1},{1,0},{2,3},{3,2},{4,5},{5,4},{6,7},{7,6},{8,9},{9,8},{10,11... | collective-permute-start | bytes 4718600 | tf_op jit(solution)/shard_map/ppermute | solution.py:632
  147.3 31.9 %collective-permute-start.12 = (bf16[128,5120]{1,0:T(8,128)(2,1)}, bf16[128,5120]{1,0:T(8,128)(2,1)}, u32[]{:S(2)}, u32[]{:S(2)}) collective-permute-start(bf16[128,5120]{1,0:T(8,128)(2,1)} %constant_dynamic-slice_fusion.1), channel_id=1, source_target_pairs={{0,8},{8,0},{16,24},{24,16},{1,9},{9,1},{17,25},{25,17},{2,10},{10... | collective-permute-start | bytes 3932168 | tf_op jit(solution)/shard_map/ppermute | solution.py:658
  148.8 33.9 %collective-permute-start.24 = (bf16[512,1024]{1,0:T(8,128)(2,1)S(1)}, bf16[512,1024]{1,0:T(8,128)(2,1)}, u32[]{:S(2)}, u32[]{:S(2)}) collective-permute-start(bf16[512,1024]{1,0:T(8,128)(2,1)S(1)} %collective-permute-done.20.rest_10_), channel_id=1, source_target_pairs={{0,1},{1,0},{2,3},{3,2},{4,5},{5,4},{6,7},{7,6},{8,9},{9,8},{10,11... | collective-permute-start | bytes 3145736 | tf_op jit(solution)/shard_map/ppermute | solution.py:663
  155.5 100.1 %collective-permute-start.31 = (bf16[128,8192]{1,0:T(8,128)(2,1)}, bf16[128,8192]{1,0:T(8,128)(2,1)S(1)}, u32[]{:S(2)}, u32[]{:S(2)}) collective-permute-start(bf16[128,8192]{1,0:T(8,128)(2,1)} %constant_dynamic-slice_fusion), channel_id=1, source_target_pairs={{0,16},{8,24},{16,0},{24,8},{1,17},{9,25},{17,1},{25,9},{2,18},{10... | collective-permute-start | bytes 6291464 | tf_op jit(solution)/shard_map/ppermute | solution.py:659
  169.1 86.7 %collective-permute-start.30 = (bf16[128,8192]{1,0:T(8,128)(2,1)}, bf16[128,8192]{1,0:T(8,128)(2,1)}, u32[]{:S(2)}, u32[]{:S(2)}) collective-permute-start(bf16[128,8192]{1,0:T(8,128)(2,1)} %constant_dynamic-slice_fusion), channel_id=1, source_target_pairs={{0,8},{8,0},{16,24},{24,16},{1,9},{9,1},{17,25},{25,17},{2,10},{10... | collective-permute-start | bytes 6291464 | tf_op jit(solution)/shard_map/ppermute | solution.py:658
  179.2 58.4 %collective-permute-start.14 = (bf16[64,5120]{1,0:T(8,128)(2,1)S(1)}, bf16[64,5120]{1,0:T(8,128)(2,1)}, u32[]{:S(2)}, u32[]{:S(2)}) collective-permute-start(bf16[64,5120]{1,0:T(8,128)(2,1)S(1)} %slice.242), channel_id=1, source_target_pairs={{0,8},{8,0},{16,24},{24,16},{1,9},{9,1},{17,25},{25,17},{2,10},{10... | collective-permute-start | bytes 1966088 | tf_op jit(solution)/shard_map/ppermute | solution.py:660
  182.7 54.9 %collective-permute-start.15 = (bf16[64,5120]{1,0:T(8,128)(2,1)}, bf16[64,5120]{1,0:T(8,128)(2,1)}, u32[]{:S(2)}, u32[]{:S(2)}) collective-permute-start(bf16[64,5120]{1,0:T(8,128)(2,1)} %slice.243), channel_id=1, source_target_pairs={{0,16},{8,24},{16,0},{24,8},{1,17},{9,25},{17,1},{25,9},{2,18},{10... | collective-permute-start | bytes 1966088 | tf_op jit(solution)/shard_map/ppermute | solution.py:661
  184.2 76.9 %collective-permute-start.16 = (bf16[128,5120]{1,0:T(8,128)(2,1)}, bf16[128,5120]{1,0:T(8,128)(2,1)}, u32[]{:S(2)}, u32[]{:S(2)}) collective-permute-start(bf16[128,5120]{1,0:T(8,128)(2,1)} %collective-permute-done.12.rest_3_.rest_1_.rest_19_), channel_id=1, source_target_pairs={{0,1},{1,0},{2,3},{3,2},{4,5},{5,4},{6,7},{7,6},{8,9},{9,8},{10,11... | collective-permute-start | bytes 3932168 | tf_op jit(solution)/shard_map/ppermute | solution.py:663
  262.6 52.1 %collective-permute-start.34 = (bf16[128,8192]{1,0:T(8,128)(2,1)}, bf16[128,8192]{1,0:T(8,128)(2,1)}, u32[]{:S(2)}, u32[]{:S(2)}) collective-permute-start(bf16[128,8192]{1,0:T(8,128)(2,1)} %collective-permute-done.30.rest_1_.rest_3_.rest_19_), channel_id=1, source_target_pairs={{0,1},{1,0},{2,3},{3,2},{4,5},{5,4},{6,7},{7,6},{8,9},{9,8},{10,11... | collective-permute-start | bytes 6291464 | tf_op jit(solution)/shard_map/ppermute | solution.py:663
  262.6 52.1 %collective-permute-start.35 = (bf16[128,8192]{1,0:T(8,128)(2,1)S(1)}, bf16[128,8192]{1,0:T(8,128)(2,1)}, u32[]{:S(2)}, u32[]{:S(2)}) collective-permute-start(bf16[128,8192]{1,0:T(8,128)(2,1)S(1)} %collective-permute-done.31.rest_2_.rest_4_.rest_20_), channel_id=1, source_target_pairs={{0,1},{1,0},{2,3},{3,2},{4,5},{5,4},{6,7},{7,6},{8,9},{9,8},{10,11... | collective-permute-start | bytes 6291464 | tf_op jit(solution)/shard_map/ppermute | solution.py:663
  285.0 29.7 %collective-permute-start.36 = (bf16[64,8192]{1,0:T(8,128)(2,1)S(1)}, bf16[64,8192]{1,0:T(8,128)(2,1)S(1)}, u32[]{:S(2)}, u32[]{:S(2)}) collective-permute-start(bf16[64,8192]{1,0:T(8,128)(2,1)S(1)} %collective-permute-done.32.rest_3_.rest_5_.rest_21_), channel_id=1, source_target_pairs={{0,1},{1,0},{2,3},{3,2},{4,5},{5,4},{6,7},{7,6},{8,9},{9,8},{10,11... | collective-permute-start | bytes 3145736 | tf_op jit(solution)/shard_map/ppermute | solution.py:663
  286.3 28.4 %collective-permute-start.37 = (bf16[64,8192]{1,0:T(8,128)(2,1)}, bf16[64,8192]{1,0:T(8,128)(2,1)S(1)}, u32[]{:S(2)}, u32[]{:S(2)}) collective-permute-start(bf16[64,8192]{1,0:T(8,128)(2,1)} %collective-permute-done.33.rest_4_.rest_6_.rest_22_), channel_id=1, source_target_pairs={{0,1},{1,0},{2,3},{3,2},{4,5},{5,4},{6,7},{7,6},{8,9},{9,8},{10,11... | collective-permute-start | bytes 3145736 | tf_op jit(solution)/shard_map/ppermute | solution.py:663
  326.6 41.5 %collective-permute-start.38 = (bf16[512,1536]{1,0:T(8,128)(2,1)}, bf16[512,1536]{1,0:T(8,128)(2,1)}, u32[]{:S(2)}, u32[]{:S(2)}) collective-permute-start(bf16[512,1536]{1,0:T(8,128)(2,1)} %get-tuple-element.54), channel_id=1, source_target_pairs={{0,1},{1,0},{2,3},{3,2},{4,5},{5,4},{6,7},{7,6},{8,9},{9,8},{10,11... | collective-permute-start | bytes 4718600 | tf_op jit(solution)/shard_map/ppermute | solution.py:632
  330.7 36.7 %collective-permute-start.50 = (bf16[256,1024]{1,0:T(8,128)(2,1)S(1)}, bf16[256,1024]{1,0:T(8,128)(2,1)S(1)}, u32[]{:S(2)}, u32[]{:S(2)}) collective-permute-start(bf16[256,1024]{1,0:T(8,128)(2,1)S(1)} %get-tuple-element.92), channel_id=1, source_target_pairs={{0,8},{1,24},{2,10},{3,26},{4,12},{5,28},{6,14},{7,30},{8,0},{9,16... | collective-permute-start | bytes 1572872 | tf_op jit(solution)/shard_map/ppermute | solution.py:610
  332.2 53.6 %collective-permute-start.51 = (bf16[256,1024]{1,0:T(8,128)(2,1)S(1)}, bf16[256,1024]{1,0:T(8,128)(2,1)S(1)}, u32[]{:S(2)}, u32[]{:S(2)}) collective-permute-start(bf16[256,1024]{1,0:T(8,128)(2,1)S(1)} %get-tuple-element.93), channel_id=1, source_target_pairs={{0,0},{1,16},{2,2},{3,18},{4,4},{5,20},{6,6},{7,22},{8,8},{9,24},{... | collective-permute-start | bytes 1572872 | tf_op jit(solution)/shard_map/ppermute | solution.py:610
  353.9 33.2 %collective-permute-start.42 = (bf16[256,1024]{1,0:T(8,128)(2,1)S(1)}, bf16[256,1024]{1,0:T(8,128)(2,1)}, u32[]{:S(2)}, u32[]{:S(2)}) collective-permute-start(bf16[256,1024]{1,0:T(8,128)(2,1)S(1)} %slice.250), channel_id=1, source_target_pairs={{0,8},{8,0},{16,24},{24,16},{1,9},{9,1},{17,25},{25,17},{2,10},{10... | collective-permute-start | bytes 1572872 | tf_op jit(solution)/shard_map/ppermute | solution.py:660
  356.1 31.0 %collective-permute-start.43 = (bf16[256,1024]{1,0:T(8,128)(2,1)S(1)}, bf16[256,1024]{1,0:T(8,128)(2,1)}, u32[]{:S(2)}, u32[]{:S(2)}) collective-permute-start(bf16[256,1024]{1,0:T(8,128)(2,1)S(1)} %slice.251), channel_id=1, source_target_pairs={{0,16},{8,24},{16,0},{24,8},{1,17},{9,25},{17,1},{25,9},{2,18},{10... | collective-permute-start | bytes 1572872 | tf_op jit(solution)/shard_map/ppermute | solution.py:661
  367.3 29.8 %collective-permute-start.44 = (bf16[512,1024]{1,0:T(8,128)(2,1)S(1)}, bf16[512,1024]{1,0:T(8,128)(2,1)S(1)}, u32[]{:S(2)}, u32[]{:S(2)}) collective-permute-start(bf16[512,1024]{1,0:T(8,128)(2,1)S(1)} %collective-permute-done.40.rest_10_), channel_id=1, source_target_pairs={{0,1},{1,0},{2,3},{3,2},{4,5},{5,4},{6,7},{7,6},{8,9},{9,8},{10,11... | collective-permute-start | bytes 3145736 | tf_op jit(solution)/shard_map/ppermute | solution.py:663
  368.1 29.0 %collective-permute-start.45 = (bf16[512,1024]{1,0:T(8,128)(2,1)S(1)}, bf16[512,1024]{1,0:T(8,128)(2,1)}, u32[]{:S(2)}, u32[]{:S(2)}) collective-permute-start(bf16[512,1024]{1,0:T(8,128)(2,1)S(1)} %collective-permute-done.41.rest_11_), channel_id=1, source_target_pairs={{0,1},{1,0},{2,3},{3,2},{4,5},{5,4},{6,7},{7,6},{8,9},{9,8},{10,11... | collective-permute-start | bytes 3145736 | tf_op jit(solution)/shard_map/ppermute | solution.py:663
  538.6 35.0 %collective-permute-start.48 = (bf16[256,1024]{1,0:T(8,128)(2,1)S(1)}, bf16[256,1024]{1,0:T(8,128)(2,1)S(1)}, u32[]{:S(2)}, u32[]{:S(2)}) collective-permute-start(bf16[256,1024]{1,0:T(8,128)(2,1)S(1)} %get-tuple-element.100), channel_id=1, source_target_pairs={{8,0},{24,1},{10,2},{26,3},{12,4},{28,5},{14,6},{30,7},{0,8},{16,9... | collective-permute-start | bytes 1572872 | tf_op jit(solution)/shard_map/ppermute | solution.py:622
  540.2 35.0 %collective-permute-start.49 = (bf16[256,1024]{1,0:T(8,128)(2,1)S(1)}, bf16[256,1024]{1,0:T(8,128)(2,1)S(1)}, u32[]{:S(2)}, u32[]{:S(2)}) collective-permute-start(bf16[256,1024]{1,0:T(8,128)(2,1)S(1)} %get-tuple-element.101), channel_id=1, source_target_pairs={{0,0},{16,1},{2,2},{18,3},{4,4},{20,5},{6,6},{22,7},{8,8},{24,9},{... | collective-permute-start | bytes 1572872 | tf_op jit(solution)/shard_map/ppermute | solution.py:622
  (82 other events, 1125.8 us)
Sparse Core Ops, SparseCore 0:
  10.2 31.7 all-gather.14
  43.7 24.5 all-gather.12
  69.9 33.3 all-gather.8
  104.8 47.5 all-gather.10
  237.7 31.5 all-gather.16

commit v2 on v1

v2 whole, which is shorter than its diff:
```python
import functools
import jax
import jax.numpy as jnp
from jax import lax
from jax.experimental import pallas as pl
from jax.experimental.pallas import tpu as pltpu
from jax.sharding import PartitionSpec as P

HEAD = 64
LANES = 128
adapter_scale = 8.0
VMEM_BYTES = 58 * 1024 * 1024
low = jnp.bfloat16
full = jnp.float32


def dot(left, right):
    return jnp.dot(left, right, preferred_element_type=full)


def dot_nt(left, right):
    return lax.dot_general(left, right, (((1,), (1,)), ((), ())), preferred_element_type=full)


def dot_tn(left, right):
    return lax.dot_general(left, right, (((0,), (0,)), ((), ())), preferred_element_type=full)


def normalise(value):
    center = value - jnp.mean(value, axis=-1, keepdims=True)
    scale = lax.rsqrt(jnp.mean(center * center, axis=-1, keepdims=True) + 1e-05)
    return center * scale, scale


def norm_back(unit, scale, gain, grad):
    grad = grad * gain
    inner = jnp.mean(grad * unit, axis=-1, keepdims=True)
    return scale * (grad - jnp.mean(grad, axis=-1, keepdims=True) - unit * inner)


def vmem():
    return pl.BlockSpec(memory_space=pltpu.VMEM)


def hbm():
    return pl.BlockSpec(memory_space=pl.ANY)


def smem():
    return pl.BlockSpec(memory_space=pltpu.SMEM)


def brief():
    return pl.CostEstimate(flops=1000, bytes_accessed=1000, transcendentals=0)


def params():
    return pltpu.CompilerParams(vmem_limit_bytes=VMEM_BYTES)


class Copies:
    def __init__(self, sems):
        self.sems, self.used, self.open = sems, 0, []

    def start(self, source, target):
        copy = pltpu.make_async_copy(source, target, self.sems.at[self.used])
        self.used += 1
        copy.start()
        return copy

    def send(self, source, target):
        self.open.append(self.start(source, target))

    def finish(self):
        for copy in self.open:
            copy.wait()

    def rows(self, pieces, column, offsets, first, target, parts=1):
        width = target.shape[1] // parts
        result = []
        for part in range(parts):
            cols = pl.ds(part * width, width)
            source = pl.ds(column + part * width, width)
            row = []
            for index, piece in enumerate(pieces):
                start = pl.multiple_of(offsets[first + index], 64)
                rows = pl.ds(start, piece.shape[0])
                row.append(self.start(piece.at[:, source], target.at[rows, cols]))
            result.append(row)
        return result


def wait_all(copies):
    for copy in copies:
        copy.wait()


def call(kernel, name, outs, scalars, small, large, scratch, sems):
    return pl.pallas_call(
        kernel,
        out_shape=outs,
        in_specs=[smem()] * len(scalars) + [vmem()] * len(small) + [hbm()] * len(large),
        out_specs=[hbm()] * len(outs),
        scratch_shapes=[pltpu.VMEM(shape, kind) for shape, kind in scratch]
        + [pltpu.SemaphoreType.DMA((sems,))],
        compiler_params=params(),
        cost_estimate=brief(),
        name=name,
    )(*scalars, *small, *large)


def sized(kind, *shape):
    return jax.ShapeDtypeStruct(shape, kind)


def project_kernel(count, column, groups, offs, gain, shift, bias, down, up, h_hbm, *rest):
    pieces, rest = rest[:count], rest[count:]
    outs, (u_hbm, a_hbm), rest = rest[:groups], rest[groups : groups + 2], rest[groups + 2 :]
    h_ref, weight, result, a_ref, u_ref, sems = rest
    move = Copies(sems)
    h_copy = move.start(h_hbm, h_ref)
    parts = 3 * groups
    loads = move.rows(pieces, column, offs, 1, weight, parts)
    member = offs[0]
    model = h_ref.shape[1]
    width = model // groups
    h_copy.wait()
    unit, _ = normalise(h_ref[...].astype(full))
    a = (unit * gain[...] + shift[...]).astype(low)
    a_ref[...] = a
    move.send(a_ref, a_hbm)
    u = dot(a, down[...]).astype(low)
    u_ref[...] = u
    move.send(u_ref, u_hbm)
    for part in range(parts):
        kind, group = part // groups, part % groups
        wait_all(loads[part])
        cols = pl.ds(part * width, width)
        value = dot(a, weight[:, cols])
        if kind != 1:
            at = pl.ds((kind // 2) * model + group * width, width)
            value = value + bias[:, at] + dot(u, up[:, at])
        result[:, cols] = value.astype(low)
        if group + 1 == groups:
            for step in range(groups):
                source = pl.multiple_of(kind * model + (member ^ step) * width, width)
                move.send(result.at[:, pl.ds(source, width)], outs[step].at[:, pl.ds(kind * width, width)])
    move.finish()


def project(offs, hidden, gain, shift, bias, down, up, pieces, groups):
    pieces, column = pieces
    tokens, model = hidden.shape
    outs = [sized(low, tokens, 3 * model // groups)] * groups
    outs += [sized(low, tokens, LANES), sized(low, tokens, model)]
    count = len(pieces)
    result = call(
        functools.partial(project_kernel, count, column, groups),
        "project",
        outs,
        [offs],
        [gain, shift, bias, down, up],
        [hidden, *pieces],
        [
            ((tokens, model), hidden.dtype),
            ((model, 3 * model), low),
            ((tokens, 3 * model), low),
            ((tokens, model), low),
            ((tokens, LANES), low),
        ],
        1 + count * 3 * groups + 2 + 3 * groups,
    )
    return result[:groups], result[groups], result[groups + 1]


def mix_kernel(count, column, groups, offs, bias, gain, shift, h_hbm, *rest):
    mixed, pieces, rest = rest[:groups], rest[groups : groups + count], rest[groups + count :]
    m_hbm, c_hbm, h_ref, o_ref, weight, m_ref, c_ref, sems = rest
    move = Copies(sems)
    width = mixed[0].shape[1]
    loads = []
    for step in range(groups):
        at = pl.multiple_of((offs[0] ^ step) * width, width)
        loads.append(move.start(mixed[step], o_ref.at[:, pl.ds(at, width)]))
    loads += move.rows(pieces, column, offs, 1, weight)[0]
    loads.append(move.start(h_hbm, h_ref))
    wait_all(loads)
    step = h_ref.shape[0] // 2
    for start in (0, step):
        rows = pl.ds(start, step)
        total = h_ref[rows, :].astype(full) + (dot(o_ref[rows, :], weight[...]) + bias[...])
        m_ref[rows, :] = total
        move.send(m_ref.at[rows, :], m_hbm.at[rows, :])
        unit, _ = normalise(total)
        c_ref[rows, :] = (unit * gain[...] + shift[...]).astype(low)
        move.send(c_ref.at[rows, :], c_hbm.at[rows, :])
    move.finish()


def mix(offs, hidden, bias, gain, shift, mixed, pieces):
    pieces, column = pieces
    groups, count = len(mixed), len(pieces)
    tokens, model = hidden.shape
    return call(
        functools.partial(mix_kernel, count, column, groups),
        "mix",
        [sized(full, tokens, model), sized(low, tokens, model)],
        [offs],
        [bias, gain, shift],
        [hidden, *mixed, *pieces],
        [
            ((tokens, model), hidden.dtype),
            ((tokens, model), low),
            ((model, model), low),
            ((tokens, model), full),
            ((tokens, model), low),
        ],
        1 + groups + count + 4,
    )


ROOT = 0.7978845608028654
CUBE = 0.044715


def feed_up_kernel(count, column, parts, offs, up_bias, c_hbm, *rest):
    pieces, (acted_hbm, slope_hbm, c_ref, up, acted, slope, sems) = rest[:count], rest[count:]
    move = Copies(sems)
    c_copy = move.start(c_hbm, c_ref)
    loads = move.rows(pieces, column, offs, 1, up, parts)
    width = up.shape[1] // parts
    c_copy.wait()
    c = c_ref[...]
    for part in range(parts):
        cols = pl.ds(part * width, width)
        wait_all(loads[part])
        z = dot(c, up[:, cols]) + up_bias[:, cols]
        square = z * z
        t = jnp.tanh(z * (ROOT + (ROOT * CUBE) * square))
        half = 0.5 + 0.5 * t
        acted[:, cols] = (z * half).astype(low)
        slope[:, cols] = (
            half + z * (1.0 - t * t) * (0.5 * ROOT + (1.5 * ROOT * CUBE) * square)
        ).astype(low)
        move.send(acted.at[:, cols], acted_hbm.at[:, cols])
        move.send(slope.at[:, cols], slope_hbm.at[:, cols])
    move.finish()


def feed_up(offs, second, up_bias, pieces):
    pieces, column = pieces
    tokens, model = second.shape
    hidden = up_bias.shape[1]
    count, parts = len(pieces), 8
    return call(
        functools.partial(feed_up_kernel, count, column, parts),
        "feed_up",
        [sized(low, tokens, hidden)] * 2,
        [offs],
        [up_bias],
        [second, *pieces],
        [
            ((tokens, model), low),
            ((model, hidden), low),
            ((tokens, hidden), low),
            ((tokens, hidden), low),
        ],
        1 + count * parts + 2 * parts,
    )


def chunks(pieces, offs, first, entries, most=512):
    if entries > len(pieces):
        rows = pieces[0].shape[0] // 4
        stripe = 128
        per = most // stripe
        for block in range(4):
            for start in range(0, rows // stripe, per):
                sources = [(0, (4 * (start + i) + block) * stripe, stripe) for i in range(per)]
                yield sources, pl.multiple_of(offs[first + block] + start * stripe, 256), most
        return
    for index, piece in enumerate(pieces):
        for start in range(0, piece.shape[0], most):
            rows = min(most, piece.shape[0] - start)
            yield [(index, start, rows)], pl.multiple_of(offs[first + index] + start, 256), rows


def load_chunk(move, pieces, sources, column, target, at):
    copies = []
    for index, start, rows in sources:
        source = pieces[index].at[pl.ds(start, rows), pl.ds(column, target.shape[1])]
        copies.append(move.start(source, target.at[pl.ds(at, rows), :]))
        at += rows
    return copies


def feed_down_kernel(count, column, entries, offs, bias, y_hbm, m_hbm, *rest):
    pieces, (h_hbm, low_hbm, y_ref, total, h_low, down, sems) = rest[:count], rest[count:]
    move = Copies(sems)
    m_copy = move.start(m_hbm, total)
    parts = []
    at = 0
    for sources, row, rows in chunks(pieces, offs, 1, entries):
        copies = [move.start(y_hbm.at[:, pl.ds(row, rows)], y_ref.at[:, pl.ds(at, rows)])]
        copies += load_chunk(move, pieces, sources, column, down, at)
        parts.append((at, rows, copies))
        at += rows
    m_copy.wait()
    total[...] += bias[...]
    for at, rows, copies in parts:
        wait_all(copies)
        total[...] += dot(y_ref[:, pl.ds(at, rows)], down[pl.ds(at, rows), :])
    move.send(total, h_hbm)
    h_low[...] = total[...].astype(low)
    move.send(h_low, low_hbm)
    move.finish()


def feed_down(offs, acted, middle, bias, pieces):
    pieces, column = pieces
    tokens, hidden = acted.shape
    model = middle.shape[1]
    count = len(pieces)
    return call(
        functools.partial(feed_down_kernel, count, column, offs.shape[0] - 1),
        "feed_down",
        [sized(full, tokens, model), sized(low, tokens, model)],
        [offs],
        [bias],
        [acted, middle, *pieces],
        [
            ((tokens, hidden), low),
            ((tokens, model), full),
            ((tokens, model), low),
            ((hidden, model), low),
        ],
        64,
    )


def feed_back_kernel(entries, ups, downs, outs_count, columns, groups, offs, gain, g_hbm, m_hbm, slope_hbm, *rest):
    up_pieces, rest = rest[:ups], rest[ups:]
    down_pieces, rest = rest[:downs], rest[downs:]
    out_pieces, rest = rest[:outs_count], rest[outs_count:]
    mid_hbm, rest = rest[0], rest[1:]
    outs, rest = rest[:groups], rest[groups:]
    g_ref, m_ref, slope, up, down, out, d_pre, d_second, mixed, sems = rest
    move = Copies(sems)
    g_copy = move.start(g_hbm, g_ref)
    parts = []
    at = 0
    for sources, row, rows in chunks(down_pieces, offs, 1 + ups, entries):
        cols, where = pl.ds(row, rows), pl.ds(at, rows)
        copies = load_chunk(move, down_pieces, sources, columns[1], down, at)
        copies.append(move.start(slope_hbm.at[:, cols], slope.at[:, where]))
        parts.append((where, cols, copies))
        at += rows
    up_loads = move.rows(up_pieces, columns[0], offs, 1, up)[0]
    m_copy = move.start(m_hbm, m_ref)
    out_loads = move.rows(out_pieces, columns[2], offs, 1 + ups + entries, out)[0]
    model = up.shape[0]
    g_copy.wait()
    g = g_ref[...].astype(low)
    for where, cols, copies in parts:
        wait_all(copies)
        d_acted = dot_nt(g, down[where, :])
        d_pre[:, cols] = (d_acted * slope[:, where].astype(full)).astype(low)
    wait_all(up_loads)
    step = 256
    for start in range(0, model, step):
        cols = pl.ds(start, step)
        d_second[:, cols] = dot_nt(d_pre[...], up[cols, :])
    m_copy.wait()
    unit, scale = normalise(m_ref[...])
    grad = g_ref[...].astype(full) + norm_back(unit, scale, gain[...], d_second[...])
    m_ref[...] = grad
    move.send(m_ref, mid_hbm)
    grad = grad.astype(low)
    wait_all(out_loads)
    width = model // groups
    for group in range(groups):
        cols = pl.ds(group * width, width)
        mixed[:, cols] = dot_nt(grad, out[cols, :]).astype(low)
    for step in range(groups):
        at = pl.multiple_of((offs[0] ^ step) * width, width)
        move.send(mixed.at[:, pl.ds(at, width)], outs[step])
    move.finish()


def feed_back(offs, grad, middle, slope, gain, up_pieces, down_pieces, out_pieces, groups):
    (up_pieces, up_column), (down_pieces, down_column) = up_pieces, down_pieces
    out_pieces, out_column = out_pieces
    columns = (up_column, down_column, out_column)
    tokens, model = middle.shape
    hidden = slope.shape[1]
    ups, downs, outs_count = len(up_pieces), len(down_pieces), len(out_pieces)
    result = call(
        functools.partial(feed_back_kernel, offs.shape[0] - 1 - ups - outs_count, ups, downs, outs_count, columns, groups),
        "feed_back",
        [sized(full, tokens, model)] + [sized(low, tokens, model // groups)] * groups,
        [offs],
        [gain],
        [grad, middle, slope, *up_pieces, *down_pieces, *out_pieces],
        [
            ((tokens, model), grad.dtype),
            ((tokens, model), full),
            ((tokens, hidden), low),
            ((model, hidden), low),
            ((hidden, model), low),
            ((model, model), low),
            ((tokens, hidden), low),
            ((tokens, model), full),
            ((tokens, model), low),
        ],
        96,
    )
    return result[0], result[1:]


def adapt_back_kernel(groups, rank, offs, up, a_hbm, u_hbm, *rest):
    grads, rest = rest[:groups], rest[groups:]
    grad_a_hbm, grad_b_hbm, d_inner_hbm, a_ref, u_ref, d_pair, d_inner, grad_a, grad_b, sems = rest
    move = Copies(sems)
    model = a_ref.shape[1]
    width = model // groups
    loads = [move.start(u_hbm, u_ref)]
    for place, kind in enumerate((0, 2)):
        for step in range(groups):
            at = pl.multiple_of(place * model + (offs[0] ^ step) * width, width)
            source = grads[step].at[:, pl.ds(kind * width, width)]
            loads.append(move.start(source, d_pair.at[:, pl.ds(at, width)]))
    a_copy = move.start(a_hbm, a_ref)
    wait_all(loads)
    d_inner[...] = dot_nt(d_pair[...], up[...]).astype(low)
    move.send(d_inner, d_inner_hbm)
    u = u_ref[...]
    lane = lax.broadcasted_iota(jnp.int32, (1, LANES), 1)
    u_query = jnp.where(lane < rank, u, 0).astype(low)
    u_value = jnp.where(lane >= rank, u, 0).astype(low)
    by_rank = dot_tn(u_query, d_pair[:, pl.ds(0, model)]) + dot_tn(u_value, d_pair[:, pl.ds(model, model)])
    grad_b[...] = adapter_scale * by_rank[:8]
    move.send(grad_b, grad_b_hbm)
    a_copy.wait()
    grad_a[...] = dot_tn(d_inner[...], a_ref[...])[:8]
    move.send(grad_a, grad_a_hbm)
    move.finish()


def adapt_back(normed, inner, up, grads, offs, rank):
    groups = len(grads)
    tokens, model = normed.shape
    return call(
        functools.partial(adapt_back_kernel, groups, rank),
        "adapt_back",
        [sized(full, 8, model), sized(full, 8, model), sized(low, tokens, LANES)],
        [offs],
        [up],
        [normed, inner, *grads],
        [
            ((tokens, model), low),
            ((tokens, LANES), low),
            ((tokens, 2 * model), low),
            ((tokens, LANES), low),
            ((8, model), full),
            ((8, model), full),
        ],
        2 + 2 * groups + 3,
    )


def project_back_kernel(count, column, groups, offs, gain, down, inner_hbm, mid_hbm, h_hbm, *rest):
    grads, pieces, rest = rest[:groups], rest[groups : groups + count], rest[groups + count :]
    g_hbm, low_hbm, d_inner, mid_ref, h_ref, weight, d_all, d_normed, g_low, sems = rest
    move = Copies(sems)
    model = h_ref.shape[1]
    width = model // groups
    loads = [move.start(inner_hbm, d_inner)]
    for kind in range(3):
        for step in range(groups):
            at = pl.multiple_of(kind * model + (offs[0] ^ step) * width, width)
            source = grads[step].at[:, pl.ds(kind * width, width)]
            loads.append(move.start(source, d_all.at[:, pl.ds(at, width)]))
    weights = move.rows(pieces, column, offs, 1, weight)[0]
    later = [move.start(h_hbm, h_ref), move.start(mid_hbm, mid_ref)]
    wait_all(loads)
    wait_all(weights)
    step = 256
    for start in range(0, model, step):
        rows = pl.ds(start, step)
        d_normed[:, rows] = dot_nt(d_all[...], weight[rows, :]) + dot_nt(d_inner[...], down[rows, :])
    wait_all(later)
    unit, scale = normalise(h_ref[...].astype(full))
    grad = mid_ref[...] + norm_back(unit, scale, gain[...], d_normed[...])
    g_low[...] = grad.astype(low)
    move.send(g_low, low_hbm)
    mid_ref[...] = grad
    move.send(mid_ref, g_hbm)
    move.finish()


def project_back(offs, mid, hidden, gain, d_inner, down, grads, pieces):
    pieces, column = pieces
    groups, count = len(grads), len(pieces)
    tokens, model = hidden.shape
    return call(
        functools.partial(project_back_kernel, count, column, groups),
        "project_back",
        [sized(full, tokens, model), sized(low, tokens, model)],
        [offs],
        [gain, down],
        [d_inner, mid, hidden, *grads, *pieces],
        [
            ((tokens, LANES), low),
            ((tokens, model), full),
            ((tokens, model), hidden.dtype),
            ((model, 3 * model), low),
            ((tokens, 3 * model), low),
            ((tokens, model), full),
            ((tokens, model), low),
        ],
        1 + 3 * groups + count + 2 + 2,
    )


def attend_kernel(groups, offs, *rest):
    pieces, rest = rest[:groups], rest[groups:]
    outs, (o_ref, lse_ref), (qkv, lse_cols, sems) = rest[:groups], rest[groups : groups + 2], rest[groups + 2 :]
    member = offs[0]
    count, width3 = pieces[0].shape
    width = width3 // 3
    length = count * groups
    pairs = width // LANES
    block = 256
    loads = []
    for step in range(groups):
        rows = pl.ds(pl.multiple_of((member ^ step) * count, count), count)
        copy = pltpu.make_async_copy(pieces[step], qkv.at[rows, :], sems.at[step])
        copy.start()
        loads.append(copy)
    for copy in loads:
        copy.wait()
    lane = lax.broadcasted_iota(jnp.int32, (1, LANES), 1)
    keep = [(lane < HEAD).astype(low), (lane >= HEAD).astype(low)]
    causal = lax.broadcasted_iota(jnp.int32, (block, block), 1) <= lax.broadcasted_iota(
        jnp.int32, (block, block), 0
    )
    lse_cols[...] = jnp.zeros_like(lse_cols)

    @pl.loop(0, pairs)
    def _(pair):
        at = pl.multiple_of(pair * LANES, LANES)
        for start in range(0, length, block):
            rows = pl.ds(start, block)
            q = qkv[rows, pl.ds(at, LANES)]
            k = qkv[pl.ds(0, start + block), pl.ds(width + at, LANES)]
            v = qkv[pl.ds(0, start + block), pl.ds(2 * width + at, LANES)]
            mixed = jnp.zeros((block, LANES), full)
            logs = lse_cols[rows, :]
            for head in range(2):
                scores = dot_nt(q * (keep[head] * 0.125), k)
                corner = jnp.where(causal, scores[:, start:], -1e30)
                if start:
                    scores = jnp.concatenate([scores[:, :start], corner], axis=1)
                else:
                    scores = corner
                top = jnp.max(scores, axis=1, keepdims=True)
                weights = jnp.exp(scores - top)
                total = jnp.sum(weights, axis=1, keepdims=True)
                part = dot(weights.astype(low), v * keep[head])
                mixed = mixed + part * (1.0 / total)
                logs = jnp.where(lane == 2 * pair + head, top + jnp.log(total), logs)
            lse_cols[rows, :] = logs
            o_ref[rows, pl.ds(at, LANES)] = mixed.astype(low)

    lse_ref[...] = lse_cols[...].T
    for step in range(groups):
        rows = pl.ds(pl.multiple_of((member ^ step) * count, count), count)
        outs[step][...] = o_ref[rows, :]


def attend(offs, pieces):
    groups = len(pieces)
    count, width3 = pieces[0].shape
    width, length = width3 // 3, count * groups
    outs = [jax.ShapeDtypeStruct((count, width), low)] * groups
    outs += [jax.ShapeDtypeStruct((length, width), low), jax.ShapeDtypeStruct((LANES, length), full)]
    result = pl.pallas_call(
        functools.partial(attend_kernel, groups),
        out_shape=outs,
        in_specs=[smem()] + [hbm()] * groups,
        out_specs=[vmem()] * len(outs),
        scratch_shapes=[
            pltpu.VMEM((length, width3), low),
            pltpu.VMEM((length, LANES), full),
            pltpu.SemaphoreType.DMA((groups,)),
        ],
        compiler_params=params(),
        cost_estimate=brief(),
        name="attend",
    )(offs, *pieces)
    return result[:groups], result[groups], result[groups + 1]


def attend_back_kernel(groups, offs, *rest):
    pieces, grads, rest = rest[:groups], rest[groups : 2 * groups], rest[2 * groups :]
    (o_ref, lse_ref), rest = rest[:2], rest[2:]
    outs, (qkv, d_out, result, inner, sems) = rest[:groups], rest[groups:]
    member = offs[0]
    count, width3 = pieces[0].shape
    width = width3 // 3
    length = count * groups
    pairs = width // LANES
    block = 256
    loads = []
    for step in range(groups):
        rows = pl.ds(pl.multiple_of((member ^ step) * count, count), count)
        for kind, (source, target) in enumerate(((pieces[step], qkv), (grads[step], d_out))):
            copy = pltpu.make_async_copy(source, target.at[rows, :], sems.at[kind, step])
            copy.start()
            loads.append(copy)
    for copy in loads:
        copy.wait()
    lane = lax.broadcasted_iota(jnp.int32, (1, LANES), 1)
    keep = [(lane < HEAD).astype(low), (lane >= HEAD).astype(low)]
    causal = lax.broadcasted_iota(jnp.int32, (block, block), 0) <= lax.broadcasted_iota(
        jnp.int32, (block, block), 1
    )
    heads = width // HEAD
    of_head = (
        lax.broadcasted_iota(jnp.int32, (max(heads, 8), width), 1) // HEAD
        == lax.broadcasted_iota(jnp.int32, (max(heads, 8), width), 0)
    ).astype(low)
    product = d_out[...].astype(full) * o_ref[...].astype(full)
    high = product.astype(low)
    rest_of = (product - high.astype(full)).astype(low)
    inner[...] = dot_nt(of_head, high) + dot_nt(of_head, rest_of)

    @pl.loop(0, pairs)
    def _(pair):
        at = pl.multiple_of(pair * LANES, LANES)
        grad_k = jnp.zeros((length, LANES), full)
        grad_v = jnp.zeros((length, LANES), full)
        for start in reversed(range(0, length, block)):
            rows = pl.ds(start, block)
            upto = start + block
            q = qkv[rows, pl.ds(at, LANES)]
            d = d_out[rows, pl.ds(at, LANES)]
            k = qkv[pl.ds(0, upto), pl.ds(width + at, LANES)]
            v = qkv[pl.ds(0, upto), pl.ds(2 * width + at, LANES)]
            grad_q = jnp.zeros((block, LANES), full)
            for head in range(2):
                q_head = q * (keep[head] * 0.125)
                d_head = d * keep[head]
                scores = dot_nt(k, q_head)
                log_sum = lse_ref[pl.ds(2 * pair + head, 1), rows]
                probs = jnp.exp(scores - log_sum)
                corner = jnp.where(causal, probs[start:], 0.0)
                probs = jnp.concatenate([probs[:start], corner], axis=0) if start else corner
                d_probs = dot_nt(v, d_head)
                d_scores = (probs * (d_probs - inner[pl.ds(2 * pair + head, 1), rows])).astype(low)
                more_v = dot(probs.astype(low), d_head)
                more_k = dot(d_scores, q_head)
                if upto < length:
                    zeros = jnp.zeros((length - upto, LANES), full)
                    more_v = jnp.concatenate([more_v, zeros], axis=0)
                    more_k = jnp.concatenate([more_k, zeros], axis=0)
                grad_v = grad_v + more_v
                grad_k = grad_k + more_k
                grad_q = grad_q + dot_tn(d_scores, k * (keep[head] * 0.125))
            result[rows, pl.ds(at, LANES)] = grad_q.astype(low)
        result[:, pl.ds(width + at, LANES)] = grad_k.astype(low)
        result[:, pl.ds(2 * width + at, LANES)] = grad_v.astype(low)

    for step in range(groups):
        rows = pl.ds(pl.multiple_of((member ^ step) * count, count), count)
        outs[step][...] = result[rows, :]


def attend_back(offs, pieces, grads, mixed, lse):
    groups = len(pieces)
    count, width3 = pieces[0].shape
    width, length = width3 // 3, count * groups
    outs = [jax.ShapeDtypeStruct((count, width3), low)] * groups
    return pl.pallas_call(
        functools.partial(attend_back_kernel, groups),
        out_shape=outs,
        in_specs=[smem()] + [hbm()] * (2 * groups) + [vmem()] * 2,
        out_specs=[vmem()] * len(outs),
        scratch_shapes=[
            pltpu.VMEM((length, width3), low),
            pltpu.VMEM((length, width), low),
            pltpu.VMEM((length, width3), low),
            pltpu.VMEM((max(width // HEAD, 8), length), full),
            pltpu.SemaphoreType.DMA((2, groups)),
        ],
        compiler_params=params(),
        cost_estimate=brief(),
        name="attend_back",
    )(offs, *pieces, *grads, mixed, lse)


def reshard_perms(sp_size, dp_size):
    quarter = sp_size // 4
    perms = []
    for part in range(2):
        perm = []
        for s in range(sp_size):
            for d in range(dp_size):
                doc = 2 * (d & 1) + ((s & 1) ^ part)
                member = s >> 1
                target_sp = doc * quarter + (member >> 1)
                target_dp = 2 * (d >> 1) + (member & 1)
                perm.append((s * dp_size + d, target_sp * dp_size + target_dp))
        perms.append(perm)
    return perms


def member_perm(sp_size, dp_size, step):
    quarter = sp_size // 4
    perm = []
    for s in range(sp_size):
        for d in range(dp_size):
            doc, high = s // quarter, s % quarter
            member = (2 * high + (d & 1)) ^ step
            target_sp = doc * quarter + (member >> 1)
            target_dp = 2 * (d >> 1) + (member & 1)
            perm.append((s * dp_size + d, target_sp * dp_size + target_dp))
    return perm


class Plan:
    def __init__(self, sp_size, dp_size):
        self.sp_size, self.dp_size = sp_size, dp_size
        self.members = sp_size // 2
        self.perms = reshard_perms(sp_size, dp_size)
        self.back = [[(b, a) for a, b in perm] for perm in self.perms]
        self.s = lax.axis_index("sp")
        self.d = lax.axis_index("dp")
        quarter = sp_size // 4
        self.doc = self.s // quarter
        self.member = 2 * (self.s % quarter) + (self.d & 1)

    def gather_start(self, blocks):
        got = []
        for part in range(2):
            block = lax.dynamic_index_in_dim(blocks, (self.s & 1) ^ part, 0, keepdims=False)
            got.append(lax.ppermute(block, ("sp", "dp"), self.perms[part]))
        return got

    def gather_finish(self, got):
        flip = (self.doc & 1) == 1
        first = jnp.where(flip, got[1], got[0])
        second = jnp.where(flip, got[0], got[1])
        return jnp.concatenate([first, second], axis=0)

    def gather_doc(self, blocks):
        return self.gather_finish(self.gather_start(blocks))

    def scatter_start(self, rows):
        half = rows.shape[0] // 2
        blocks = rows.reshape(2, half, rows.shape[1])
        got = []
        for part in range(2):
            block = lax.dynamic_index_in_dim(blocks, (self.doc & 1) ^ part, 0, keepdims=False)
            got.append(lax.ppermute(block, ("sp", "dp"), self.back[part]))
        return got

    def scatter_finish(self, got):
        flip = (self.s & 1) == 1
        first = jnp.where(flip, got[1], got[0])
        second = jnp.where(flip, got[0], got[1])
        return jnp.stack([first, second])

    def scatter_doc(self, rows):
        return self.scatter_finish(self.scatter_start(rows))

    def swap(self, parts):
        out = [parts[0]]
        for step in range(1, self.members):
            perm = member_perm(self.sp_size, self.dp_size, step)
            out.append(lax.ppermute(parts[step], ("sp", "dp"), perm))
        return out


def all_sum(value, sp_size, dp_size):
    total = sp_size * dp_size
    step = 1
    while step < total:
        value = value + lax.ppermute(
            value, ("sp", "dp"), [(i, i ^ step) for i in range(total)]
        )
        step *= 2
    return value


def after(value, *earlier):
    return lax.optimization_barrier((value, *earlier))[0]


class Clock:
    def __init__(self):
        self.event = ()

    def tick(self, *values):
        self.event = values

    def tied(self, *values):
        if not self.event:
            return values if len(values) > 1 else values[0]
        got = lax.optimization_barrier((*values, *self.event))[: len(values)]
        return got if len(values) > 1 else got[0]


class Fetch:
    def __init__(self, plan, clock, shard):
        self.plan, self.clock = plan, clock
        self.whole = plan.sp_size != 4
        shard = clock.tied(shard)
        if self.whole:
            self.block = lax.all_gather(shard, ("sp", "dp"), axis=0, tiled=True)
            self.side = self.corner = self.block
            return
        self.block = lax.all_gather(shard, "dp", axis=0, tiled=True)
        sp_size, dp_size = plan.sp_size, plan.dp_size
        self.over_core = [(i, i ^ 1) for i in range(dp_size)]
        places = [(s, d) for s in range(sp_size) for d in range(dp_size)]
        self.first_way = [(s * dp_size + d, (s ^ (1 << (d & 1))) * dp_size + d) for s, d in places]
        self.second_way = [(s * dp_size + d, (s ^ (2 >> (d & 1))) * dp_size + d) for s, d in places]

    def near(self):
        if not self.whole:
            block = self.clock.tied(self.block)
            self.side = lax.ppermute(block, ("sp", "dp"), self.first_way)

    def far(self):
        if self.whole:
            return
        rows = self.block.shape[0]
        self.side = self.clock.tied(self.side)
        half = lax.dynamic_slice_in_dim(self.side, (self.plan.d & 1) * (rows // 2), rows // 2, axis=0)
        self.corner = lax.ppermute(half, ("sp", "dp"), self.second_way)
        self.other_side = lax.ppermute(self.side, "dp", self.over_core)

    def pieces(self):
        plan = self.plan
        if self.whole:
            return [self.block], [0]
        corner = self.clock.tied(self.corner)
        other_corner = lax.ppermute(corner, "dp", self.over_core)
        rows = self.block.shape[0]
        s, core = plan.s, plan.d & 1
        half = rows // 2
        starts = [
            s * rows,
            (s ^ (1 << core)) * rows,
            (s ^ (2 >> core)) * rows,
            (s ^ 3) * rows + core * half,
            (s ^ 3) * rows + (1 - core) * half,
        ]
        return [self.block, self.side, self.other_side, corner, other_corner], starts


class Wide:
    def __init__(self, plan, clock, shard):
        self.plan, self.clock = plan, clock
        self.whole = plan.sp_size != 4
        shard = clock.tied(shard)
        self.parts = [shard]
        if not self.whole:
            for step in range(1, 4):
                way = [(i, i ^ step) for i in range(4)]
                self.parts.append(lax.ppermute(shard, "sp", way))

    def gather(self):
        parts = self.clock.tied(*self.parts) if len(self.parts) > 1 else self.parts
        axes = ("sp", "dp") if self.whole else "dp"
        self.block = lax.all_gather(jnp.concatenate(parts), axes, axis=0, tiled=True)

    def pieces(self):
        if self.whole:
            return [self.block], [0]
        rows = self.block.shape[0] // 4
        return [self.block], [(self.plan.s ^ step) * rows for step in range(4)]


def on_device(
    tokens,
    cotangent,
    layer_norm_gain,
    layer_norm_bias,
    query_key_value_weight,
    query_value_bias,
    attention_out_weight,
    output_projection_bias,
    feed_up_weight,
    feed_up_bias,
    feed_down_weight,
    adapter_down_maps,
    adapter_up_weights,
):
    layers = query_key_value_weight.shape[0]
    model = tokens.shape[2]
    rank = adapter_down_maps.shape[3]
    plan = Plan(lax.axis_size("sp"), lax.axis_size("dp"))
    clock = Clock()
    groups = plan.members
    member = plan.member.astype(jnp.int32)

    def table(*entries):
        return jnp.stack([jnp.asarray(entry, jnp.int32) for entry in entries])

    adapters = []
    for layer in range(layers):
        down = jnp.concatenate([adapter_down_maps[layer, 0], adapter_down_maps[layer, 1]], axis=1)
        down = jnp.pad(down, ((0, 0), (0, LANES - 2 * rank)))
        up = adapter_up_weights[layer] * jnp.asarray(adapter_scale, low)
        up = jnp.concatenate(
            [
                jnp.pad(up[0], ((0, LANES - rank), (0, 0))),
                jnp.pad(up[1], ((rank, LANES - 2 * rank), (0, 0))),
            ],
            axis=1,
        )
        adapters.append((down, up))

    def request(layer, kind):
        if layer == layers:
            return None
        if (layer, kind) == (layers - 1, 2):
            wide.gather()
            wide.side = wide.block
            return wide
        if kind == 0:
            shard = query_key_value_weight[layer]
        elif kind == 1:
            shard = jnp.concatenate([attention_out_weight[layer], feed_up_weight[layer]], axis=1)
        else:
            shard = feed_down_weight[layer]
        return Fetch(plan, clock, shard)

    saved, outputs = [], []
    ready = {}
    qkv_fetch = request(0, 0)
    hidden = plan.gather_doc(tokens)
    clock.tick(hidden)
    out_fetch = request(0, 1)
    down_fetch = request(0, 2)
    wide = Wide(plan, clock, feed_down_weight[layers - 1])
    clock.tick(*wide.parts)
    qkv_fetch.near()
    clock.tick(hidden)
    qkv_fetch.far()
    clock.tick(qkv_fetch.side)
    out_fetch.near()
    for layer in range(layers):
        last = layer + 1 == layers
        gain, shift = layer_norm_gain[layer], layer_norm_bias[layer]
        down, up = adapters[layer]
        clock.tick(hidden, qkv_fetch.corner)
        ready[layer, 0] = qkv_fetch.pieces()
        qkv, starts = ready[layer, 0]
        offs = table(member, *starts)
        bias = query_value_bias[layer].reshape(1, 2 * model)
        clock.tick(out_fetch.block)
        next_qkv = request(layer + 1, 0)
        parts, inner, normed = project(
            offs, clock.tied(hidden), gain[:1], shift[:1], bias, down, up, (qkv, 0), groups
        )
        clock.tick(*parts)
        out_fetch.far()
        parts = plan.swap(parts)
        clock.tick(out_fetch.side)
        if not last:
            down_fetch.near()
        parts[0] = clock.tied(parts[0])
        mixed_parts, mixed, lse = attend(offs, parts)
        clock.tick(mixed)
        next_out = request(layer + 1, 1)
        mixed_parts = plan.swap(mixed_parts)
        clock.tick(mixed, out_fetch.corner)
        next_down = request(layer + 1, 2)
        if last:
            sent = plan.gather_start(after(cotangent, mixed))
        ready[layer, 1] = out_fetch.pieces()
        out_up, starts = ready[layer, 1]
        if not last:
            clock.tick(down_fetch.side)
            mixed_parts[0] = clock.tied(mixed_parts[0])
        offs = table(member, *starts)
        middle, second = mix(
            offs,
            hidden,
            output_projection_bias[layer, :1],
            gain[1:],
            shift[1:],
            mixed_parts,
            (out_up, 0),
        )
        if not last:
            down_fetch.far()
            clock.tick(down_fetch.side)
            next_qkv.near()
            clock.tick(next_qkv.block)
        acted, slope = feed_up(
            offs, clock.tied(second), feed_up_bias[layer : layer + 1], (out_up, model)
        )
        clock.tick(acted)
        if last:
            sent = clock.tied(*sent)
            grad = plan.gather_finish(sent)
        else:
            next_out.near()
            clock.tick(acted, down_fetch.corner)
        ready[layer, 2] = down_fetch.pieces()
        saved.append((hidden, normed, inner, parts, mixed, lse, middle, acted, slope))
        down_w, starts = ready[layer, 2]
        if not last:
            clock.tick(next_out.block)
            hidden, after_low = feed_down(
                table(member, *starts),
                clock.tied(acted),
                middle,
                output_projection_bias[layer, 1:],
                (down_w, 0),
            )
            clock.tick(hidden)
            next_qkv.far()
            outputs.append(plan.scatter_start(after_low))
            qkv_fetch, out_fetch, down_fetch = next_qkv, next_out, next_down
    sums = [None] * layers
    waiting = outputs.pop()
    for layer in reversed(range(layers)):
        hidden, normed, inner, parts, mixed, lse, middle, acted, slope = saved[layer]
        gain = layer_norm_gain[layer]
        down, up = adapters[layer]
        (qkv, starts), (out_up, starts_up) = ready[layer, 0], ready[layer, 1]
        down_w, starts_down = ready[layer, 2]
        offs = table(member, *starts)
        mid, d_mixed = feed_back(
            table(member, *starts_up, *starts_down, *starts_up),
            grad,
            middle,
            slope,
            gain[1:],
            (out_up, model),
            (down_w, 0),
            (out_up, 0),
            groups,
        )
        d_mixed = plan.swap(d_mixed)
        if layer + 1 == layers:
            _, after_low = feed_down(
                table(member, *starts_down),
                after(acted, mid),
                middle,
                output_projection_bias[layer, 1:],
                (down_w, 0),
            )
            outputs_late = [plan.scatter_start(after_low)]
            d_mixed[0] = after(d_mixed[0], after_low)
        grads = list(attend_back(offs, parts, d_mixed, mixed, lse))
        if waiting:
            grads[1], *arrived = lax.optimization_barrier((grads[1], *waiting))
            outputs.append(arrived)
        if outputs_late:
            waiting = outputs_late.pop()
        else:
            waiting = []
        grads = plan.swap(grads)
        grad_a, grad_b, d_inner = adapt_back(normed, inner, up, grads, offs, rank)
        grad, grad_low = project_back(
            offs, mid, hidden, gain[:1], after(d_inner, grad_a), down, grads, (qkv, 0)
        )
        sums[layer] = jnp.concatenate([grad_a, grad_b])
    total = all_sum(jnp.stack(sums), plan.sp_size, plan.dp_size).reshape(layers, 2, 8, model)[:, :, : 2 * rank]
    total = total.reshape(layers, 2, 2, rank, model)
    grad_tokens = plan.scatter_doc(grad_low).astype(full)
    outputs = [plan.scatter_finish(got).astype(full) for got in outputs]
    return (jnp.stack(outputs), grad_tokens, total[:, 0].swapaxes(-1, -2), total[:, 1])


def solution(mesh):
    in_specs = (
        P("dp", "sp", None),
        P("dp", "sp", None),
        P(),
        P(),
        P(None, ("sp", "dp"), None),
        P(),
        P(None, ("sp", "dp"), None),
        P(),
        P(None, ("sp", "dp"), None),
        P(),
        P(None, ("sp", "dp"), None),
        P(),
        P(),
    )
    out_specs = (P(None, "dp", "sp", None), P("dp", "sp", None), P(), P())
    return jax.shard_map(
        on_device, mesh=mesh, in_specs=in_specs, out_specs=out_specs, check_vma=False
    )
```

time: 605 us -> 486 us (0.80)
  waiting for transfers between devices: 239 us -> 145 us
  starting transfers between devices: 59.7 us -> 46.3 us
  local copies, waits for them, and re-layouts: 43.8 us -> 31.7 us
    all_gather x5 -> x6, waiting for transfers between devices: 50.7 us -> 4.43 us  [the longest x5 4.43 us: __init__(): self.block = lax.all_gather(shard, 'dp', axis=0, tiled=True)]
    ppermute x50 -> x33, waiting for transfers between devices: 163 us -> 120 us  [the longest x5 50.4 us: near(): self.side = lax.ppermute(block, ('sp', 'dp'), self.first_way)]
    ppermute x50 -> x33, starting transfers between devices: 43.5 us -> 32 us  [the longest x4 10 us: gather_start(): got.append(lax.ppermute(block, ('sp', 'dp'), self.perms[part]))]
    slice x13 -> x1, local copies, waits for them, and re-layouts: 12.5 us -> 1.44 us  [on_device(): shift[1:]]
    ppermute x10 -> x5, starting transfers between devices: 13.8 us -> 6.25 us  [all_sum(): lax.ppermute(value, ('sp', 'dp'), [(i, i ^ step) for i in range(total)])]
    ppermute x10 -> x5, waiting for transfers between devices: 17.4 us -> 13.4 us  [all_sum(): lax.ppermute(value, ('sp', 'dp'), [(i, i ^ step) for i in range(total)])]
    pallas_call x10 -> x14, Pallas kernels: 149 us -> 147 us  [call(): pl.pallas_call(kernel, out_shape=outs, in_specs=[smem()] * len(scalars) +...]
  transfers between devices with their start and end apart: 73 -> 52, of which waited for: 23 -> 20; matrix products, arithmetic and copies ran while one was open for 7% -> 8% of each run, Pallas kernels for 17% -> 35%
where the time goes in v2:
time: 486 us; the launch traced here: 478 us
  Pallas kernels  226 us (47%)
  waiting for transfers between devices  145 us (30%)
  starting transfers between devices  46.3 us (10%)
  local copies, waits for them, and re-layouts  31.7 us (7%)
  between operations  15.2 us (3%)
  other arithmetic  13.4 us (3%)
    pallas_call x14, Pallas kernels, call(): pl.pallas_call(kernel, out_shape=outs, in_specs=[smem()] * len(scalars) +...  147 us
    ppermute x5, waiting for transfers between devices, near(): self.side = lax.ppermute(block, ('sp', 'dp'), self.first_way)  50.4 us
    ppermute x5, waiting for transfers between devices, far(): self.corner = lax.ppermute(half, ('sp', 'dp'), self.second_way)  46.5 us
    pallas_call x2, Pallas kernels, attend_back(): pl.pallas_call(functools.partial(attend_back_kernel, groups), out_shape=o...  44.1 us
    pallas_call x2, Pallas kernels, attend(): pl.pallas_call(functools.partial(attend_kernel, groups), out_shape=outs,...  35.1 us
    ppermute x5, waiting for transfers between devices, all_sum(): lax.ppermute(value, ('sp', 'dp'), [(i, i ^ step) for i in range(total)])  13.4 us
    ppermute x3, waiting for transfers between devices, __init__(): self.parts.append(lax.ppermute(shard, 'sp', way))  11.7 us
    ppermute x4, starting transfers between devices, gather_start(): got.append(lax.ppermute(block, ('sp', 'dp'), self.perms[part]))  10 us
  transfers between devices with their start and end apart: 52, of which 20 were waited for; matrix products, arithmetic and copies ran while one was open for 8% of the time, Pallas kernels for 35%

profile of v2, /device:TPU:0, one launch (start us, length us, event | category | flops | bytes accessed | tf_op | source)
XLA Modules:
  0.0 477.7 jit_solution(4613557125636720747)
XLA Ops:
  15.7 9.8 %collective-permute-done = bf16[256,1024]{1,0:T(8,128)(2,1)S(1)} collective-permute-done((bf16[256,1024]{1,0:T(8,128)(2,1)S(1)}, bf16[256,1024]{1,0:T(8,128)(2,1)S(1)}, u32[]{:S(2)}, u32[]{:S(2)}) %collective-permute-start) | collective-permute-done | bytes 524320 | tf_op jit(solution)/shard_map/ppermute | solution.py:747
  27.5 4.6 collective-permute-start.4
  33.1 5.8 %collective-permute-done.4 = bf16[128,1024]{1,0:T(8,128)(2,1)S(1)} collective-permute-done((bf16[128,1024]{1,0:T(8,128)(2,1)S(1)}, bf16[128,1024]{1,0:T(8,128)(2,1)S(1)}, u32[]{:S(2)}, u32[]{:S(2)}) %collective-permute-start.4) | collective-permute-done | bytes 262176 | tf_op jit(solution)/shard_map/ppermute | solution.py:872
  38.9 6.0 %collective-permute-done.3 = bf16[128,1024]{1,0:T(8,128)(2,1)S(1)} collective-permute-done((bf16[128,1024]{1,0:T(8,128)(2,1)S(1)}, bf16[128,1024]{1,0:T(8,128)(2,1)S(1)}, u32[]{:S(2)}, u32[]{:S(2)}) %collective-permute-start.3) | collective-permute-done | bytes 262176 | tf_op jit(solution)/shard_map/ppermute | solution.py:872
  46.0 19.7 %collective-permute-done.5.rest_1_.rest_3_ = bf16[256,3072]{1,0:T(8,128)(2,1)} collective-permute-done((bf16[256,3072]{1,0:T(8,128)(2,1)}, bf16[256,3072]{1,0:T(8,128)(2,1)}, u32[]{:S(2)}, u32[]{:S(2)}) %collective-permute-start.5) | collective-permute-done | bytes 1572896 | tf_op jit(solution)/shard_map/ppermute | solution.py:833
  69.3 4.4 all-gather.8.cloned.1.call-done.rest_2_.rest_0_.rest_10_
  76.0 7.2 %collective-permute-done.7.rest_3_.rest_5_ = bf16[128,3072]{1,0:T(8,128)(2,1)S(1)} collective-permute-done((bf16[128,3072]{1,0:T(8,128)(2,1)}, bf16[128,3072]{1,0:T(8,128)(2,1)S(1)}, u32[]{:S(2)}, u32[]{:S(2)}) %collective-permute-start.7) | collective-permute-done | bytes 786464 | tf_op jit(solution)/shard_map/ppermute | solution.py:841
  89.5 9.5 %project.2 = (bf16[512,1536]{1,0:T(8,128)(2,1)}, bf16[512,1536]{1,0:T(8,128)(2,1)}, bf16[512,128]{1,0:T(8,128)(2,1)}, bf16[512,1024]{1,0:T(8,128)(2,1)}) custom-call(s32[6]{0:T(128)} %stack.73.offs, f32[1,1024]{1,0:T(1,128)} %get-tuple-element.244.gain, f32[1,1024]{1,0:T(1,128)} %get-tuple-element.229.shift, f32[1,2048]{1,0:T(1,128)} %bitcast.131, ...), custom_call_target="tpu_custom_call" | custom-call | flops 1000 | bytes 1000 | tf_op jit(solution)/shard_map/project/pallas_call | solution.py:99
  100.3 6.0 %collective-permute-done.9.rest_3_.rest_1_.rest_11_ = bf16[256,5120]{1,0:T(8,128)(2,1)S(1)} collective-permute-done((bf16[256,5120]{1,0:T(8,128)(2,1)}, bf16[256,5120]{1,0:T(8,128)(2,1)S(1)}, u32[]{:S(2)}, u32[]{:S(2)}) %collective-permute-start.9) | collective-permute-done | bytes 2621472 | tf_op jit(solution)/shard_map/ppermute | solution.py:833
  106.3 17.7 %attend.2 = (bf16[512,512]{1,0:T(8,128)(2,1)}, bf16[512,512]{1,0:T(8,128)(2,1)}, bf16[1024,512]{1,0:T(8,128)(2,1)}, f32[128,1024]{1,0:T(8,128)}) custom-call(s32[6]{0:T(128)} %stack.73.offs, bf16[512,1536]{1,0:T(8,128)(2,1)} %get-tuple-element.104.rest_0_, bf16[512,1536]{1,0:T(8,128)(2,1)} %collective-permute-done.10.rest_1_), custom_call_target="tpu_custom_call" | custom-call | flops 1000 | bytes 1000 | tf_op jit(solution)/shard_map/attend/pallas_call | solution.py:587
  125.4 16.7 %collective-permute-done.14.rest_5_.rest_3_.rest_13_ = bf16[128,5120]{1,0:T(8,128)(2,1)} collective-permute-done((bf16[128,5120]{1,0:T(8,128)(2,1)S(1)}, bf16[128,5120]{1,0:T(8,128)(2,1)}, u32[]{:S(2)}, u32[]{:S(2)}) %collective-permute-start.14) | collective-permute-done | bytes 1310752 | tf_op jit(solution)/shard_map/ppermute | solution.py:841
  145.0 24.7 %collective-permute-done.11.rest_1_.rest_6_ = bf16[1024,1024]{1,0:T(8,128)(2,1)} collective-permute-done((bf16[1024,1024]{1,0:T(8,128)(2,1)}, bf16[1024,1024]{1,0:T(8,128)(2,1)}, u32[]{:S(2)}, u32[]{:S(2)}) %collective-permute-start.11) | collective-permute-done | bytes 2097184 | tf_op jit(solution)/shard_map/ppermute | solution.py:833
  174.7 6.2 %mix.2 = (f32[512,1024]{1,0:T(8,128)}, bf16[512,1024]{1,0:T(8,128)(2,1)}) custom-call(s32[6]{0:T(128)} %stack.73.offs, f32[1,1024]{1,0:T(1,128)} %get-tuple-element.223.bias, f32[1,1024]{1,0:T(1,128)} %get-tuple-element.246.gain, f32[1,1024]{1,0:T(1,128)} %get-tuple-element.227.shift, bf16[512,1024]{1,0:T(8,128)(2,1)} %pad_maximum_fusion.h_hbm, ...), custom_call_target="tpu_custom_call" | custom-call | flops 1000 | bytes 1000 | tf_op jit(solution)/shard_map/mix/pallas_call | solution.py:99
  180.9 13.1 %feed_up.2 = (bf16[512,4096]{1,0:T(8,128)(2,1)}, bf16[512,4096]{1,0:T(8,128)(2,1)}) custom-call(s32[6]{0:T(128)} %stack.73.offs, f32[1,4096]{1,0:T(1,128)} %get-tuple-element.215.up_bias, bf16[512,1024]{1,0:T(8,128)(2,1)} %get-tuple-element.114.c_hbm, bf16[256,5120]{1,0:T(8,128)(2,1)} %all-gather.8.cloned.1.call-done.rest_2_.rest_0_.rest_10_, ...), custom_call_target="tpu_custom_call" | custom-call | flops 1000 | bytes 1000 | tf_op jit(solution)/shard_map/feed_up/pallas_call | solution.py:99
  200.0 10.3 %feed_down.2 = (f32[512,1024]{1,0:T(8,128)}, bf16[512,1024]{1,0:T(8,128)(2,1)}) custom-call(s32[6]{0:T(128)} %stack.79.offs, f32[1,1024]{1,0:T(1,128)} %get-tuple-element.224.bias, bf16[512,4096]{1,0:T(8,128)(2,1)} %get-tuple-element.117.y_hbm, f32[512,1024]{1,0:T(8,128)} %get-tuple-element.118.m_hbm, ...), custom_call_target="tpu_custom_call" | custom-call | flops 1000 | bytes 1000 | tf_op jit(solution)/shard_map/feed_down/pallas_call | solution.py:99
  212.3 19.7 %collective-permute-done.21.rest_3_.rest_5_ = bf16[128,3072]{1,0:T(8,128)(2,1)S(1)} collective-permute-done((bf16[128,3072]{1,0:T(8,128)(2,1)S(1)}, bf16[128,3072]{1,0:T(8,128)(2,1)S(1)}, u32[]{:S(2)}, u32[]{:S(2)}) %collective-permute-start.21) | collective-permute-done | bytes 786464 | tf_op jit(solution)/shard_map/ppermute | solution.py:841
  236.2 9.8 %project.3 = (bf16[512,1536]{1,0:T(8,128)(2,1)}, bf16[512,1536]{1,0:T(8,128)(2,1)}, bf16[512,128]{1,0:T(8,128)(2,1)}, bf16[512,1024]{1,0:T(8,128)(2,1)}) custom-call(s32[6]{0:T(128)} %stack.73.offs, f32[1,1024]{1,0:T(1,128)} %get-tuple-element.245.gain, f32[1,1024]{1,0:T(1,128)} %get-tuple-element.228.shift, f32[1,2048]{1,0:T(1,128)} %bitcast.130, ...), custom_call_target="tpu_custom_call" | custom-call | flops 1000 | bytes 1000 | tf_op jit(solution)/shard_map/project/pallas_call | solution.py:99
  251.0 17.4 %attend.3 = (bf16[512,512]{1,0:T(8,128)(2,1)}, bf16[512,512]{1,0:T(8,128)(2,1)}, bf16[1024,512]{1,0:T(8,128)(2,1)}, f32[128,1024]{1,0:T(8,128)}) custom-call(s32[6]{0:T(128)} %stack.73.offs, bf16[512,1536]{1,0:T(8,128)(2,1)} %get-tuple-element.130.rest_0_, bf16[512,1536]{1,0:T(8,128)(2,1)} %copy-done.4), custom_call_target="tpu_custom_call" | custom-call | flops 1000 | bytes 1000 | tf_op jit(solution)/shard_map/attend/pallas_call | solution.py:587
  270.9 5.5 %collective-permute-start.25 = (bf16[256,1024]{1,0:T(8,128)(2,1)}, bf16[256,1024]{1,0:T(8,128)(2,1)}, u32[]{:S(2)}, u32[]{:S(2)}) collective-permute-start(bf16[256,1024]{1,0:T(8,128)(2,1)} %get-tuple-element.199), channel_id=1, source_target_pairs={{0,0},{1,16},{2,2},{3,18},{4,4},{5,20},{6,6},{7,22},{8,8},{9,24},{... | collective-permute-start | bytes 1572872 | tf_op jit(solution)/shard_map/ppermute | solution.py:747
  277.0 6.4 %mix.3 = (f32[512,1024]{1,0:T(8,128)}, bf16[512,1024]{1,0:T(8,128)(2,1)}) custom-call(s32[6]{0:T(128)} %stack.73.offs, f32[1,1024]{1,0:T(1,128)} %get-tuple-element.225.bias, f32[1,1024]{1,0:T(1,128)} %get-tuple-element.247.gain, f32[1,1024]{1,0:T(1,128)} %get-tuple-element.226.shift, f32[512,1024]{1,0:T(8,128)} %get-tuple-element.122.h_hbm, ...), custom_call_target="tpu_custom_call" | custom-call | flops 1000 | bytes 1000 | tf_op jit(solution)/shard_map/mix/pallas_call | solution.py:99
  283.4 13.1 %feed_up.3 = (bf16[512,4096]{1,0:T(8,128)(2,1)}, bf16[512,4096]{1,0:T(8,128)(2,1)}) custom-call(s32[6]{0:T(128)} %stack.73.offs, f32[1,4096]{1,0:T(1,128)} %get-tuple-element.214.up_bias, bf16[512,1024]{1,0:T(8,128)(2,1)} %get-tuple-element.137.c_hbm, bf16[256,5120]{1,0:T(8,128)(2,1)} %all-gather.14.cloned.1.call-done.rest_2_.rest_0_.rest_6_, ...), custom_call_target="tpu_custom_call" | custom-call | flops 1000 | bytes 1000 | tf_op jit(solution)/shard_map/feed_up/pallas_call | solution.py:99
  298.7 17.9 %feed_back.2 = (f32[512,1024]{1,0:T(8,128)}, bf16[512,512]{1,0:T(8,128)(2,1)}, bf16[512,512]{1,0:T(8,128)(2,1)}) custom-call(s32[15]{0:T(128)} %stack.83.offs, f32[1,1024]{1,0:T(1,128)} %get-tuple-element.247.gain, bf16[512,1024]{1,0:T(8,128)(2,1)} %pad_maximum_fusion.1.g_hbm, f32[512,1024]{1,0:T(8,128)} %get-tuple-element.141.m_hbm, ...), custom_call_target="tpu_custom_call" | custom-call | flops 1000 | bytes 1000 | tf_op jit(solution)/shard_map/feed_back/pallas_call | solution.py:99
  319.3 9.8 %feed_down.3 = (f32[512,1024]{1,0:T(8,128)}, bf16[512,1024]{1,0:T(8,128)(2,1)}) custom-call(s32[5]{0:T(128)} %stack.84.offs, f32[1,1024]{1,0:T(1,128)} %get-tuple-element.222.bias, bf16[512,4096]{1,0:T(8,128)(2,1)} %get-tuple-element.149.y_hbm, f32[512,1024]{1,0:T(8,128)} %get-tuple-element.141.m_hbm, ...), custom_call_target="tpu_custom_call" | custom-call | flops 1000 | bytes 1000 | tf_op jit(solution)/shard_map/feed_down/pallas_call | solution.py:99
  329.9 22.1 %attend_back.2 = (bf16[512,1536]{1,0:T(8,128)(2,1)}, bf16[512,1536]{1,0:T(8,128)(2,1)}) custom-call(s32[6]{0:T(128)} %stack.73.offs, bf16[512,1536]{1,0:T(8,128)(2,1)} %get-tuple-element.130.rest_0_, bf16[512,1536]{1,0:T(8,128)(2,1)} %copy-done.4, bf16[512,512]{1,0:T(8,128)(2,1)} %get-tuple-element.151.rest_2_, bf16[512,512]{1,0:T(8,128)(2,1)} %copy-done.13, ...), custom_call_target="tpu_custom_call" | custom-call | flops 1000 | bytes 1000 | tf_op jit(solution)/shard_map/attend_back/pallas_call | solution.py:684
  359.4 4.9 %adapt_back.2 = (f32[8,1024]{1,0:T(8,128)}, f32[8,1024]{1,0:T(8,128)}, bf16[512,128]{1,0:T(8,128)(2,1)}) custom-call(s32[6]{0:T(128)} %stack.73.offs, bf16[128,2048]{1,0:T(8,128)(2,1)} %fusion.4.up, bf16[512,1024]{1,0:T(8,128)(2,1)} %get-tuple-element.158.a_hbm, bf16[512,128]{1,0:T(8,128)(2,1)} %get-tuple-element.159.u_hbm, ...), custom_call_target="tpu_custom_call" | custom-call | flops 1000 | bytes 1000 | tf_op jit(solution)/shard_map/adapt_back/pallas_call | solution.py:99
  364.3 11.5 %project_back.2 = (f32[512,1024]{1,0:T(8,128)}, bf16[512,1024]{1,0:T(8,128)(2,1)}) custom-call(s32[6]{0:T(128)} %stack.73.offs, f32[1,1024]{1,0:T(1,128)} %get-tuple-element.245.gain, bf16[1024,128]{1,0:T(8,128)(2,1)} %pad.21.down, bf16[512,128]{1,0:T(8,128)(2,1)} %get-tuple-element.164.inner_hbm, f32[512,1024]{1,0:T(8,128)} %get-tuple-element.148.mid_hbm, ...), custom_call_target="tpu_custom_call" | custom-call | flops 1000 | bytes 1000 | tf_op jit(solution)/shard_map/project_back/pallas_call | solution.py:99
  375.8 18.0 %feed_back.3 = (f32[512,1024]{1,0:T(8,128)}, bf16[512,512]{1,0:T(8,128)(2,1)}, bf16[512,512]{1,0:T(8,128)(2,1)}) custom-call(s32[16]{0:T(128)} %stack.88.offs, f32[1,1024]{1,0:T(1,128)} %get-tuple-element.246.gain, f32[512,1024]{1,0:T(8,128)} %get-tuple-element.165.g_hbm, f32[512,1024]{1,0:T(8,128)} %get-tuple-element.118.m_hbm, ...), custom_call_target="tpu_custom_call" | custom-call | flops 1000 | bytes 1000 | tf_op jit(solution)/shard_map/feed_back/pallas_call | solution.py:99
  396.9 22.0 %attend_back.3 = (bf16[512,1536]{1,0:T(8,128)(2,1)}, bf16[512,1536]{1,0:T(8,128)(2,1)}) custom-call(s32[6]{0:T(128)} %stack.73.offs, bf16[512,1536]{1,0:T(8,128)(2,1)} %get-tuple-element.104.rest_0_, bf16[512,1536]{1,0:T(8,128)(2,1)} %collective-permute-done.10.rest_1_, bf16[512,512]{1,0:T(8,128)(2,1)} %get-tuple-element.167.rest_2_, ...), custom_call_target="tpu_custom_call" | custom-call | flops 1000 | bytes 1000 | tf_op jit(solution)/shard_map/attend_back/pallas_call | solution.py:684
  425.8 4.9 %adapt_back.3 = (f32[8,1024]{1,0:T(8,128)}, f32[8,1024]{1,0:T(8,128)}, bf16[512,128]{1,0:T(8,128)(2,1)}) custom-call(s32[6]{0:T(128)} %stack.73.offs, bf16[128,2048]{1,0:T(8,128)(2,1)} %fusion.5.up, bf16[512,1024]{1,0:T(8,128)(2,1)} %get-tuple-element.173.a_hbm, bf16[512,128]{1,0:T(8,128)(2,1)} %get-tuple-element.174.u_hbm, ...), custom_call_target="tpu_custom_call" | custom-call | flops 1000 | bytes 1000 | tf_op jit(solution)/shard_map/adapt_back/pallas_call | solution.py:99
  432.0 11.6 %project_back.3 = (f32[512,1024]{1,0:T(8,128)}, bf16[512,1024]{1,0:T(8,128)(2,1)}) custom-call(s32[6]{0:T(128)} %stack.73.offs, f32[1,1024]{1,0:T(1,128)} %get-tuple-element.244.gain, bf16[1024,128]{1,0:T(8,128)(2,1)} %pad.24.down, bf16[512,128]{1,0:T(8,128)(2,1)} %get-tuple-element.179.inner_hbm, f32[512,1024]{1,0:T(8,128)} %get-tuple-element.180.mid_hbm, ...), custom_call_target="tpu_custom_call" | custom-call | flops 1000 | bytes 1000 | tf_op jit(solution)/shard_map/project_back/pallas_call | solution.py:99
  452.0 7.1 %collective-permute-done.43 = f32[2,16,1024]{2,1,0:T(8,128)S(1)} collective-permute-done((f32[2,16,1024]{2,1,0:T(8,128)S(1)}, f32[2,16,1024]{2,1,0:T(8,128)S(1)}, u32[]{:S(2)}, u32[]{:S(2)}) %collective-permute-start.43) | collective-permute-done | bytes 131104 | tf_op jit(solution)/shard_map/ppermute | solution.py:789
  466.4 3.4 collective-permute-done.45
  (217 shorter events, 96.0 us)
Async XLA Ops:
  7.2 37.7 %all-gather.18.cloned.1.call-start = ((), (), s32[]{:S(2)}) async-start(), calls=%async_computation.5 | async-start | bytes 1769472 | tf_op jit(solution)/shard_map/all_gather | solution.py:823
  9.1 64.6 %all-gather.8.cloned.1.call-start = ((), (), s32[]{:S(2)}) async-start(), calls=%async_computation | async-start | bytes 2949120 | tf_op jit(solution)/shard_map/all_gather | solution.py:823
  10.4 15.0 %collective-permute-start = (bf16[256,1024]{1,0:T(8,128)(2,1)S(1)}, bf16[256,1024]{1,0:T(8,128)(2,1)S(1)}, u32[]{:S(2)}, u32[]{:S(2)}) collective-permute-start(bf16[256,1024]{1,0:T(8,128)(2,1)S(1)} %get-tuple-element.202), channel_id=1, source_target_pairs={{0,8},{1,24},{2,10},{3,26},{4,12},{5,28},{6,14},{7,30},{8,0},{9,16... | collective-permute-start | bytes 1572872 | tf_op jit(solution)/shard_map/ppermute | solution.py:747
  26.7 116.7 %all-gather.10.cloned.1.call-start = ((), (), s32[]{:S(2)}) async-start(), calls=%async_computation.1 | async-start | bytes 2359296 | tf_op jit(solution)/shard_map/all_gather | solution.py:823
  27.5 142.3 %all-gather.12.cloned.1.call-start = ((), (), s32[]{:S(2)}) async-start(), calls=%async_computation.2 | async-start | bytes 1769472 | tf_op jit(solution)/shard_map/all_gather | solution.py:823
  44.9 20.8 %collective-permute-start.5 = (bf16[256,3072]{1,0:T(8,128)(2,1)}, bf16[256,3072]{1,0:T(8,128)(2,1)}, u32[]{:S(2)}, u32[]{:S(2)}) collective-permute-start(bf16[256,3072]{1,0:T(8,128)(2,1)} %bitcast.124), channel_id=1, source_target_pairs={{0,8},{1,17},{2,10},{3,19},{4,12},{5,21},{6,14},{7,23},{8,0},{9,25... | collective-permute-start | bytes 4718600 | tf_op jit(solution)/shard_map/ppermute | solution.py:833
  67.8 15.3 %collective-permute-start.7 = (bf16[128,3072]{1,0:T(8,128)(2,1)}, bf16[128,3072]{1,0:T(8,128)(2,1)S(1)}, u32[]{:S(2)}, u32[]{:S(2)}) collective-permute-start(bf16[128,3072]{1,0:T(8,128)(2,1)} %constant_dynamic-slice_fusion.4), channel_id=1, source_target_pairs={{0,16},{1,9},{2,18},{3,11},{4,20},{5,13},{6,22},{7,15},{8,24},{9,1... | collective-permute-start | bytes 2359304 | tf_op jit(solution)/shard_map/ppermute | solution.py:841
  68.7 20.8 %collective-permute-start.6 = (bf16[256,3072]{1,0:T(8,128)(2,1)}, bf16[256,3072]{1,0:T(8,128)(2,1)}, u32[]{:S(2)}, u32[]{:S(2)}) collective-permute-start(bf16[256,3072]{1,0:T(8,128)(2,1)} %collective-permute-done.5.rest_1_.rest_3_), channel_id=1, source_target_pairs={{0,1},{1,0},{2,3},{3,2},{4,5},{5,4},{6,7},{7,6},{8,9},{9,8},{10,11... | collective-permute-start | bytes 4718600 | tf_op jit(solution)/shard_map/ppermute | solution.py:842
  73.7 32.6 %collective-permute-start.9 = (bf16[256,5120]{1,0:T(8,128)(2,1)}, bf16[256,5120]{1,0:T(8,128)(2,1)S(1)}, u32[]{:S(2)}, u32[]{:S(2)}) collective-permute-start(bf16[256,5120]{1,0:T(8,128)(2,1)} %all-gather.8.cloned.1.call-done.rest_2_.rest_0_.rest_10_), channel_id=1, source_target_pairs={{0,8},{1,17},{2,10},{3,19},{4,12},{5,21},{6,14},{7,23},{8,0},{9,25... | collective-permute-start | bytes 7864328 | tf_op jit(solution)/shard_map/ppermute | solution.py:833
  75.3 121.6 %all-gather.14.cloned.1.call-start = ((), (), s32[]{:S(2)}) async-start(), calls=%async_computation.3 | async-start | bytes 2949120 | tf_op jit(solution)/shard_map/all_gather | solution.py:823
  124.0 174.7 %all-gather.16.cloned.1.call-start = ((), (), s32[]{:S(2)}) async-start(), calls=%async_computation.4 | async-start | bytes 9437184 | tf_op jit(solution)/shard_map/all_gather | solution.py:877
  124.4 17.8 %collective-permute-start.14 = (bf16[128,5120]{1,0:T(8,128)(2,1)S(1)}, bf16[128,5120]{1,0:T(8,128)(2,1)}, u32[]{:S(2)}, u32[]{:S(2)}) collective-permute-start(bf16[128,5120]{1,0:T(8,128)(2,1)S(1)} %constant_dynamic-slice_fusion.3), channel_id=1, source_target_pairs={{0,16},{1,9},{2,18},{3,11},{4,20},{5,13},{6,22},{7,15},{8,24},{9,1... | collective-permute-start | bytes 3932168 | tf_op jit(solution)/shard_map/ppermute | solution.py:841
  143.3 26.4 %collective-permute-start.11 = (bf16[1024,1024]{1,0:T(8,128)(2,1)}, bf16[1024,1024]{1,0:T(8,128)(2,1)}, u32[]{:S(2)}, u32[]{:S(2)}) collective-permute-start(bf16[1024,1024]{1,0:T(8,128)(2,1)} %all-gather.10.cloned.1.call-done.rest_0_.rest_5_), channel_id=1, source_target_pairs={{0,8},{1,17},{2,10},{3,19},{4,12},{5,21},{6,14},{7,23},{8,0},{9,25... | collective-permute-start | bytes 6291464 | tf_op jit(solution)/shard_map/ppermute | solution.py:833
  144.4 30.3 %collective-permute-start.13 = (bf16[256,5120]{1,0:T(8,128)(2,1)S(1)}, bf16[256,5120]{1,0:T(8,128)(2,1)}, u32[]{:S(2)}, u32[]{:S(2)}) collective-permute-start(bf16[256,5120]{1,0:T(8,128)(2,1)S(1)} %collective-permute-done.9.rest_3_.rest_1_.rest_11_), channel_id=1, source_target_pairs={{0,1},{1,0},{2,3},{3,2},{4,5},{5,4},{6,7},{7,6},{8,9},{9,8},{10,11... | collective-permute-start | bytes 7864328 | tf_op jit(solution)/shard_map/ppermute | solution.py:842
  144.5 27.6 %collective-permute-start.12 = (bf16[512,512]{1,0:T(8,128)(2,1)}, bf16[512,512]{1,0:T(8,128)(2,1)S(1)}, u32[]{:S(2)}, u32[]{:S(2)}) collective-permute-start(bf16[512,512]{1,0:T(8,128)(2,1)} %get-tuple-element.109), channel_id=1, source_target_pairs={{0,1},{1,0},{2,3},{3,2},{4,5},{5,4},{6,7},{7,6},{8,9},{9,8},{10,11... | collective-permute-start | bytes 1572872 | tf_op jit(solution)/shard_map/ppermute | solution.py:781
  144.9 29.8 %collective-permute-start.15 = (bf16[128,5120]{1,0:T(8,128)(2,1)}, bf16[128,5120]{1,0:T(8,128)(2,1)}, u32[]{:S(2)}, u32[]{:S(2)}) collective-permute-start(bf16[128,5120]{1,0:T(8,128)(2,1)} %collective-permute-done.14.rest_5_.rest_3_.rest_13_), channel_id=1, source_target_pairs={{0,1},{1,0},{2,3},{3,2},{4,5},{5,4},{6,7},{7,6},{8,9},{9,8},{10,11... | collective-permute-start | bytes 3932168 | tf_op jit(solution)/shard_map/ppermute | solution.py:849
  169.8 30.3 %collective-permute-start.16 = (bf16[1024,1024]{1,0:T(8,128)(2,1)}, bf16[1024,1024]{1,0:T(8,128)(2,1)}, u32[]{:S(2)}, u32[]{:S(2)}) collective-permute-start(bf16[1024,1024]{1,0:T(8,128)(2,1)} %collective-permute-done.11.rest_1_.rest_6_), channel_id=1, source_target_pairs={{0,1},{1,0},{2,3},{3,2},{4,5},{5,4},{6,7},{7,6},{8,9},{9,8},{10,11... | collective-permute-start | bytes 6291464 | tf_op jit(solution)/shard_map/ppermute | solution.py:842
  171.1 25.8 %collective-permute-start.17 = (bf16[512,1024]{1,0:T(8,128)(2,1)S(1)}, bf16[512,1024]{1,0:T(8,128)(2,1)}, u32[]{:S(2)}, u32[]{:S(2)}) collective-permute-start(bf16[512,1024]{1,0:T(8,128)(2,1)S(1)} %constant_dynamic-slice_fusion.2), channel_id=1, source_target_pairs={{0,16},{1,9},{2,18},{3,11},{4,20},{5,13},{6,22},{7,15},{8,24},{9,1... | collective-permute-start | bytes 3145736 | tf_op jit(solution)/shard_map/ppermute | solution.py:841
  172.1 38.2 %collective-permute-start.19 = (bf16[256,3072]{1,0:T(8,128)(2,1)}, bf16[256,3072]{1,0:T(8,128)(2,1)}, u32[]{:S(2)}, u32[]{:S(2)}) collective-permute-start(bf16[256,3072]{1,0:T(8,128)(2,1)} %all-gather.12.cloned.1.call-done.rest_0_.rest_2_), channel_id=1, source_target_pairs={{0,8},{1,17},{2,10},{3,19},{4,12},{5,21},{6,14},{7,23},{8,0},{9,25... | collective-permute-start | bytes 4718600 | tf_op jit(solution)/shard_map/ppermute | solution.py:833
  196.8 49.7 %collective-permute-start.23 = (bf16[256,5120]{1,0:T(8,128)(2,1)}, bf16[256,5120]{1,0:T(8,128)(2,1)S(1)}, u32[]{:S(2)}, u32[]{:S(2)}) collective-permute-start(bf16[256,5120]{1,0:T(8,128)(2,1)} %all-gather.14.cloned.1.call-done.rest_2_.rest_0_.rest_6_), channel_id=1, source_target_pairs={{0,8},{1,17},{2,10},{3,19},{4,12},{5,21},{6,14},{7,23},{8,0},{9,25... | collective-permute-start | bytes 7864328 | tf_op jit(solution)/shard_map/ppermute | solution.py:833
  211.5 20.5 %collective-permute-start.21 = (bf16[128,3072]{1,0:T(8,128)(2,1)S(1)}, bf16[128,3072]{1,0:T(8,128)(2,1)S(1)}, u32[]{:S(2)}, u32[]{:S(2)}) collective-permute-start(bf16[128,3072]{1,0:T(8,128)(2,1)S(1)} %constant_dynamic-slice_fusion.1), channel_id=1, source_target_pairs={{0,16},{1,9},{2,18},{3,11},{4,20},{5,13},{6,22},{7,15},{8,24},{9,1... | collective-permute-start | bytes 2359304 | tf_op jit(solution)/shard_map/ppermute | solution.py:841
  212.1 24.1 %collective-permute-start.20 = (bf16[256,3072]{1,0:T(8,128)(2,1)}, bf16[256,3072]{1,0:T(8,128)(2,1)}, u32[]{:S(2)}, u32[]{:S(2)}) collective-permute-start(bf16[256,3072]{1,0:T(8,128)(2,1)} %collective-permute-done.19.rest_1_.rest_3_), channel_id=1, source_target_pairs={{0,1},{1,0},{2,3},{3,2},{4,5},{5,4},{6,7},{7,6},{8,9},{9,8},{10,11... | collective-permute-start | bytes 4718600 | tf_op jit(solution)/shard_map/ppermute | solution.py:842
  247.8 20.6 %collective-permute-start.29 = (bf16[128,5120]{1,0:T(8,128)(2,1)}, bf16[128,5120]{1,0:T(8,128)(2,1)}, u32[]{:S(2)}, u32[]{:S(2)}) collective-permute-start(bf16[128,5120]{1,0:T(8,128)(2,1)} %constant_dynamic-slice_fusion), channel_id=1, source_target_pairs={{0,16},{1,9},{2,18},{3,11},{4,20},{5,13},{6,22},{7,15},{8,24},{9,1... | collective-permute-start | bytes 3932168 | tf_op jit(solution)/shard_map/ppermute | solution.py:841
  248.3 28.7 %collective-permute-start.28 = (bf16[256,5120]{1,0:T(8,128)(2,1)S(1)}, bf16[256,5120]{1,0:T(8,128)(2,1)}, u32[]{:S(2)}, u32[]{:S(2)}) collective-permute-start(bf16[256,5120]{1,0:T(8,128)(2,1)S(1)} %collective-permute-done.23.rest_3_.rest_1_.rest_7_), channel_id=1, source_target_pairs={{0,1},{1,0},{2,3},{3,2},{4,5},{5,4},{6,7},{7,6},{8,9},{9,8},{10,11... | collective-permute-start | bytes 7864328 | tf_op jit(solution)/shard_map/ppermute | solution.py:842
  270.1 26.4 %collective-permute-start.26 = (bf16[256,1024]{1,0:T(8,128)(2,1)}, bf16[256,1024]{1,0:T(8,128)(2,1)S(1)}, u32[]{:S(2)}, u32[]{:S(2)}) collective-permute-start(bf16[256,1024]{1,0:T(8,128)(2,1)} %get-tuple-element.198), channel_id=1, source_target_pairs={{0,8},{1,24},{2,10},{3,26},{4,12},{5,28},{6,14},{7,30},{8,0},{9,16... | collective-permute-start | bytes 1572872 | tf_op jit(solution)/shard_map/ppermute | solution.py:747
  270.9 25.6 %collective-permute-start.25 = (bf16[256,1024]{1,0:T(8,128)(2,1)}, bf16[256,1024]{1,0:T(8,128)(2,1)}, u32[]{:S(2)}, u32[]{:S(2)}) collective-permute-start(bf16[256,1024]{1,0:T(8,128)(2,1)} %get-tuple-element.199), channel_id=1, source_target_pairs={{0,0},{1,16},{2,2},{3,18},{4,4},{5,20},{6,6},{7,22},{8,8},{9,24},{... | collective-permute-start | bytes 1572872 | tf_op jit(solution)/shard_map/ppermute | solution.py:747
  316.7 35.3 %collective-permute-start.33 = (bf16[256,1024]{1,0:T(8,128)(2,1)S(1)}, bf16[256,1024]{1,0:T(8,128)(2,1)S(1)}, u32[]{:S(2)}, u32[]{:S(2)}) collective-permute-start(bf16[256,1024]{1,0:T(8,128)(2,1)S(1)} %get-tuple-element.194), channel_id=1, source_target_pairs={{8,0},{24,1},{10,2},{26,3},{12,4},{28,5},{14,6},{30,7},{0,8},{16,9... | collective-permute-start | bytes 1572872 | tf_op jit(solution)/shard_map/ppermute | solution.py:765
  318.0 34.0 %collective-permute-start.32 = (bf16[256,1024]{1,0:T(8,128)(2,1)S(1)}, bf16[256,1024]{1,0:T(8,128)(2,1)S(1)}, u32[]{:S(2)}, u32[]{:S(2)}) collective-permute-start(bf16[256,1024]{1,0:T(8,128)(2,1)S(1)} %get-tuple-element.195), channel_id=1, source_target_pairs={{0,0},{16,1},{2,2},{18,3},{4,4},{20,5},{6,6},{22,7},{8,8},{24,9},{... | collective-permute-start | bytes 1572872 | tf_op jit(solution)/shard_map/ppermute | solution.py:765
  394.4 24.5 %collective-permute-start.37 = (bf16[256,1024]{1,0:T(8,128)(2,1)S(1)}, bf16[256,1024]{1,0:T(8,128)(2,1)S(1)}, u32[]{:S(2)}, u32[]{:S(2)}) collective-permute-start(bf16[256,1024]{1,0:T(8,128)(2,1)S(1)} %get-tuple-element.192), channel_id=1, source_target_pairs={{8,0},{24,1},{10,2},{26,3},{12,4},{28,5},{14,6},{30,7},{0,8},{16,9... | collective-permute-start | bytes 1572872 | tf_op jit(solution)/shard_map/ppermute | solution.py:765
  395.3 23.6 %collective-permute-start.36 = (bf16[256,1024]{1,0:T(8,128)(2,1)S(1)}, bf16[256,1024]{1,0:T(8,128)(2,1)S(1)}, u32[]{:S(2)}, u32[]{:S(2)}) collective-permute-start(bf16[256,1024]{1,0:T(8,128)(2,1)S(1)} %get-tuple-element.193), channel_id=1, source_target_pairs={{0,0},{16,1},{2,2},{18,3},{4,4},{20,5},{6,6},{22,7},{8,8},{24,9},{... | collective-permute-start | bytes 1572872 | tf_op jit(solution)/shard_map/ppermute | solution.py:765
  446.6 18.2 %collective-permute-start.39 = (bf16[256,1024]{1,0:T(8,128)(2,1)S(1)}, bf16[256,1024]{1,0:T(8,128)(2,1)S(1)}, u32[]{:S(2)}, u32[]{:S(2)}) collective-permute-start(bf16[256,1024]{1,0:T(8,128)(2,1)S(1)} %get-tuple-element.186), channel_id=1, source_target_pairs={{8,0},{24,1},{10,2},{26,3},{12,4},{28,5},{14,6},{30,7},{0,8},{16,9... | collective-permute-start | bytes 1572872 | tf_op jit(solution)/shard_map/ppermute | solution.py:765
  447.6 17.2 %collective-permute-start.40 = (bf16[256,1024]{1,0:T(8,128)(2,1)S(1)}, bf16[256,1024]{1,0:T(8,128)(2,1)S(1)}, u32[]{:S(2)}, u32[]{:S(2)}) collective-permute-start(bf16[256,1024]{1,0:T(8,128)(2,1)S(1)} %get-tuple-element.187), channel_id=1, source_target_pairs={{0,0},{16,1},{2,2},{18,3},{4,4},{20,5},{6,6},{22,7},{8,8},{24,9},{... | collective-permute-start | bytes 1572872 | tf_op jit(solution)/shard_map/ppermute | solution.py:765
  (52 other events, 787.2 us)
Sparse Core Ops, SparseCore 0:
  10.2 27.7 all-gather.17
  40.2 33.3 all-gather.7
  75.3 28.2 all-gather.9
  105.0 25.6 all-gather.11
  132.3 33.3 all-gather.13
  167.1 83.0 all-gather.15
